TPU v7x, 256 devices: a whole 4x4x8 slice. The times are simulated.
256 devices in a mesh: sec: 64 (over x, z_lo, y, core), op: 4 (over z_hi).
Axes of the slice: x: 4, y: 4, z: 8 (z_hi: 4, z_lo: 2; z = z_hi * 2 + z_lo), core: 2. Of those that a mesh axis runs over, the one named last changes fastest.
Arguments:
- psi: bfloat16 [64, 512, 512], P('sec', 'op'), may hold values from -6 to 6
- left_ops: bfloat16 [24, 64, 512, 512], P(None, 'sec', None, 'op'), may hold values from -0.0546875 to 0.0546875
- right_ops: bfloat16 [24, 64, 512, 512], P(None, 'sec', 'op'), may hold values from -0.25 to 0.25
- sources: int32 [64, 24], P('sec'), may hold values from 0 to 63
- counts: int32 [64], P('sec'), may hold values from 6 to 24, as said below
- dims_left: int32 [64], P('sec'), may hold values from 128 to 512, as said below
- dims_right: int32 [64], P('sec'), may hold values from 128 to 512, as said below
Outputs:
- sigma: bfloat16 [64, 512, 512], P('sec', 'op')
Inputs may be any that keep to these rules, and one draw needn't show every extreme that they name: `counts`: some sector has all 24 terms active. `dims_left`: some sector has the full padded dimension. `dims_right`: some sector has the full padded dimension.
All inputs are finite; a program needn't handle non-finite values.
Results may differ from a plain program's by a relative error of at most 0.0049.
Values may be sent and summed in bfloat16 or wider, within the bound.
No kernel may reach another device: no remote copies, remote signals or barrier semaphores. Data moves between devices by JAX's collectives and lax.ppermute only.
A program may use at most 128 MiB of HBM per device.

v0:
```python
import jax
import jax.numpy as jnp
from jax import lax
from jax.sharding import PartitionSpec as P


def body(psi, left_ops, right_ops, sources, counts, dims_left, dims_right):
    row_count = psi.shape[1]
    col_count = psi.shape[2]
    term_count = left_ops.shape[0]
    op_index = lax.axis_index("op")
    row_ids = op_index * row_count + lax.broadcasted_iota(jnp.int32, (row_count, col_count), 0)
    col_ids = lax.broadcasted_iota(jnp.int32, (row_count, col_count), 1)
    inside_mask = (row_ids < dims_left[0]) & (col_ids < dims_right[0])
    panel = jnp.where(inside_mask, psi[0], jnp.zeros_like(psi[0]))[None]
    sources_here = sources[0]
    all_panels = lax.all_gather(panel, "sec", axis=0, tiled=True)
    chosen = jnp.take(all_panels, sources_here, axis=0)
    image = jnp.einsum(
        "kab,kcb->kac",
        chosen,
        lax.all_gather(right_ops, "op", axis=2, tiled=True)[:, 0],
        preferred_element_type=jnp.float32,
    )
    active = jnp.arange(term_count, dtype=jnp.int32) < counts[0]
    image = jnp.where(active[:, None, None], image, jnp.zeros_like(image)).astype(jnp.bfloat16)
    partial_sum = jnp.einsum(
        "kab,kbc->ac", left_ops[:, 0], image, preferred_element_type=jnp.float32
    )
    reduced = lax.psum_scatter(partial_sum[None], "op", scatter_dimension=1, tiled=True)
    return jnp.where(inside_mask[None], reduced, jnp.zeros_like(reduced)).astype(jnp.bfloat16)


def solution(mesh):
    return jax.shard_map(
        body,
        mesh=mesh,
        in_specs=(
            P("sec", "op", None),
            P(None, "sec", None, "op"),
            P(None, "sec", "op", None),
            P("sec", None),
            P("sec"),
            P("sec"),
            P("sec"),
        ),
        out_specs=P("sec", "op", None),
        check_vma=False,
    )
```

profile of v0, /device:TPU:1, one launch (start us, length us, event | category | flops | bytes accessed | tf_op | source)
XLA Modules:
  0.0 406.2 jit_solution(4516154097357937161)
XLA Ops:
  6.5 0.0 copy-start
  6.5 0.0 copy-start.1
  6.5 0.0 all-gather.3.cloned.1.call-start
  8.2 1.0 copy.10
  9.2 0.1 and_select_fusion.1
  9.4 0.8 copy.11
  10.1 0.0 all-gather.3.cloned.1.call-update
  10.2 0.0 all-gather.5.cloned.1.call-start
  10.2 0.7 all-gather.5.cloned.1.call-update
  10.9 0.0 reduce-scatter.2.cloned.1.call-start
  11.6 0.0 copy-done.1
  11.7 116.5 %all-gather.3.cloned.1.call-done = bf16[64,128,512]{2,1,0:T(8,128)(2,1)} async-done(((bf16[1,128,512]{2,1,0:T(8,128)(2,1)}), bf16[64,128,512]{2,1,0:T(8,128)(2,1)}) %all-gather.3.cloned.1.call-update) | async-done | bytes 8388624 | tf_op jit(solution)/shard_map/all_gather | solution.py:17
  128.1 5.9 %gather_fusion = bf16[24,128,512]{2,1,0:T(8,128)(2,1)} fusion(bf16[64,128,512]{2,1,0:T(8,128)(2,1)} %all-gather.3.cloned.1.call-done, s32[1024]{0:T(1024)S(1)} %pad_clamp_fusion), kind=kCustom, calls=%fused_computation | custom fusion | bytes 6291552 | tf_op jit(solution)/shard_map/jit(_take)/gather | solution.py:18
  134.0 220.3 %all-gather.5.cloned.1.call-done = bf16[24,1,512,512]{3,2,1,0:T(8,128)(2,1)} async-done(((bf16[24,1,128,512]{3,2,1,0:T(8,128)(2,1)}), bf16[24,1,512,512]{3,2,1,0:T(8,128)(2,1)}) %all-gather.5.cloned.1.call-update) | async-done | bytes 12582928 | tf_op jit(solution)/shard_map/all_gather | solution.py:22
  354.3 0.0 copy-done
  354.3 11.7 %fusion.17 = f32[1,512,512]{1,2,0:T(8,128)} fusion(bf16[24,1,512,128]{3,2,1,0:T(8,128)(2,1)S(1)} %copy-done, pred[24]{0:T(512)(128)(4,1)S(1)} %get-tuple-element.6, bf16[24,1,512,512]{3,2,1,0:T(8,128)(2,1)} %all-gather.5.cloned.1.call-done, bf16[24,128,512]{2,1,0:T(8,128)(2,1)} %gather_fusion, pred[24]{0:T(512)(128)(4,1)S(1)} %get-tuple-element.5), kind=kOutput, calls=%fused_computation.11 | convolution fusion | flops 3225944064 | bytes 19922992 | tf_op jit(solution)/shard_map/kab,kbc->ac/dot_general | solution.py:27
  366.0 0.0 reduce-scatter.2.cloned.1.call-update
  366.1 31.7 %reduce-scatter.2.cloned.1.call-done = f32[1,128,512]{1,2,0:T(8,128)} async-done(((f32[1,512,512]{1,2,0:T(8,128)}), f32[1,128,512]{1,2,0:T(8,128)}) %reduce-scatter.2.cloned.1.call-update) | async-done | bytes 262160 | tf_op jit(solution)/shard_map/reduce_scatter | solution.py:30
  397.8 1.1 fusion.24
  398.9 0.8 copy.12
  (5 shorter events, 0.0 us)
Async XLA Ops:
  6.5 347.8 %copy-start = (bf16[24,1,512,128]{3,2,1,0:T(8,128)(2,1)S(1)}, bf16[24,1,512,128]{3,2,1,0:T(8,128)(2,1)}, u32[]{:S(2)}) copy-start(bf16[24,1,512,128]{3,2,1,0:T(8,128)(2,1)} %param.8) | copy-start | bytes 9437188
  6.5 5.1 %copy-start.1 = (s32[1,24]{1,0:T(1,128)S(1)}, s32[1,24]{1,0:T(1,128)}, u32[]{:S(2)}) copy-start(s32[1,24]{1,0:T(1,128)} %param.10) | copy-start | bytes 292
  6.5 121.6 %all-gather.3.cloned.1.call-start = ((), (), s32[]{:S(2)}) async-start(), calls=%async_computation.1 | async-start | bytes 8519680 | tf_op jit(solution)/shard_map/all_gather | solution.py:17
  10.2 344.2 %all-gather.5.cloned.1.call-start = ((), (), s32[]{:S(2)}) async-start(), calls=%async_computation.2 | async-start | bytes 15728640 | tf_op jit(solution)/shard_map/all_gather | solution.py:22
  10.9 386.9 %reduce-scatter.2.cloned.1.call-start = ((), (), s32[]{:S(2)}) async-start(), calls=%async_computation.3 | async-start | bytes 1310720 | tf_op jit(solution)/shard_map/reduce_scatter | solution.py:30
Sparse Core Ops, SparseCore 0:
  10.3 117.8 all-gather.2
  130.0 224.3 all-gather.4
  366.2 31.5 reduce-scatter.1
where the time goes:
time: 406 us
  waiting for transfers between devices  369 us (91%)
  between operations  15.4 us (4%)
  matrix products  11.7 us (3%)
  local copies, waits for them, and re-layouts  8.46 us (2%)
    all_gather x1, waiting for transfers between devices, body(): lax.all_gather(right_ops, 'op', axis=2, tiled=True)[:, 0]  220 us
    all_gather x1, waiting for transfers between devices, body(): all_panels = lax.all_gather(panel, 'sec', axis=0, tiled=True)  116 us
    reduce_scatter x1, waiting for transfers between devices, body(): lax.psum_scatter(partial_sum[None], 'op', scatter_dimension=1, tiled=True)  31.7 us
    dot_general x1, matrix products, body(): jnp.einsum('kab,kbc->ac', left_ops[:, 0], image, preferred_element_type=j...  11.7 us
  transfers between devices with their start and end apart: 3, of which 3 were waited for; matrix products, arithmetic and copies ran while one was open for 1% of the time, Pallas kernels for 0%

commit v1 on v0

v1 whole, which is shorter than its diff:
```python
import functools

import jax
import jax.numpy as jnp
from jax import lax
from jax.experimental import pallas as pl
from jax.experimental.pallas import tpu as pltpu
from jax.sharding import Mesh
from jax.sharding import PartitionSpec as P

NX, NL, NY, NC, NZ = 4, 2, 4, 2, 4
F32, BF16 = jnp.float32, jnp.bfloat16
SEC = ("x", "l", "y", "c")
SHARE = 4
WIRE = BF16
VMEM_LIMIT = 40 * 1024 * 1024
ANY = pl.BlockSpec(memory_space=pl.ANY)
SMEM = pl.BlockSpec(memory_space=pltpu.SMEM)
VMEM = pl.BlockSpec(memory_space=pltpu.VMEM)
PARAMS = pltpu.CompilerParams(vmem_limit_bytes=VMEM_LIMIT)


def along(value, which, step):
    perm = []
    for x in range(NX):
        for y in range(NY):
            for c in range(NC):
                on_y = (c == 0) == (which == 0)
                far = (x, (y + step) % NY) if on_y else ((x + step) % NX, y)
                perm.append(((far[0] * NY + far[1]) * NC + c, (x * NY + y) * NC + c))
    return lax.ppermute(value, ("x", "y", "c"), perm)


def swap(value, axis):
    return lax.ppermute(value, axis, [(0, 1), (1, 0)])


def from_op(value, step):
    return lax.ppermute(value, "z", [((z + step) % NZ, z) for z in range(NZ)])


def after(value, *others):
    return lax.optimization_barrier((value,) + others)[0]


def fetch(k, at, facts, pieces, panels, sems):
    own_pieces, other_pieces = pieces[:2], pieces[2:]
    for number, piece in enumerate(own_pieces):

        @pl.when(facts[0, k] == number)
        def _():
            pltpu.make_async_copy(piece.at[pl.ds(facts[1, k], 1)], panels.at[at, pl.ds(0, 1)], sems.at[at, 0]).start()

    for number, piece in enumerate(other_pieces):

        @pl.when(facts[2, k] == number)
        def _():
            pltpu.make_async_copy(piece.at[pl.ds(facts[3, k], NZ - 1)], panels.at[at, pl.ds(1, NZ - 1)], sems.at[at, 1]).start()


def fetched(at, pieces, panels, sems):
    pltpu.make_async_copy(pieces[0].at[pl.ds(0, 1)], panels.at[at, pl.ds(0, 1)], sems.at[at, 0]).wait()
    pltpu.make_async_copy(pieces[2].at[pl.ds(0, NZ - 1)], panels.at[at, pl.ds(1, NZ - 1)], sems.at[at, 1]).wait()


def product(panel, right, active):
    panel = panel.reshape(panel.shape[0] * panel.shape[1], panel.shape[2])
    value = lax.dot_general(panel, right, (((1,), (1,)), ((), ())), preferred_element_type=F32)
    return jnp.where(active, value, jnp.zeros_like(value)).astype(BF16)


def moving_kernel(first, place_ref, facts, count_ref, right_ref, *rest):
    pieces = rest[:18]
    out_ref, panels, rights, panel_sems, right_sem = rest[18:]
    terms = out_ref.shape[1]
    rights_copy = pltpu.make_async_copy(right_ref.at[pl.ds(first, terms)], rights, right_sem)
    rights_copy.start()

    def start(t, carry):
        fetch(first + t, t, facts, pieces, panels, panel_sems)
        return carry

    lax.fori_loop(0, terms, start, 0)
    rights_copy.wait()

    def step(pair, carry):
        for inner in range(2):
            fetched(pair * 2 + inner, pieces, panels, panel_sems)
        for inner in range(2):
            t = pair * 2 + inner
            value = product(panels[t], rights[t], first + t < count_ref[0])
            rows = value.shape[0] // NZ
            for j in range(NZ):
                out_ref[lax.rem(place_ref[0] + j, NZ), t] = value[j * rows : (j + 1) * rows]
        return carry

    lax.fori_loop(0, terms // 2, step, 0)


def moving_products(first, place, facts, count, right, pieces):
    terms, cols, depth = right.shape
    terms -= first
    return pl.pallas_call(
        functools.partial(moving_kernel, first),
        out_shape=jax.ShapeDtypeStruct((NZ, terms, cols, cols), BF16),
        in_specs=[SMEM] * 3 + [ANY] * 19,
        out_specs=VMEM,
        scratch_shapes=[
            pltpu.VMEM((terms, NZ, cols, depth), BF16),
            pltpu.VMEM((terms, cols, depth), BF16),
            pltpu.SemaphoreType.DMA((terms, 2)),
            pltpu.SemaphoreType.DMA,
        ],
        compiler_params=PARAMS,
        cost_estimate=pl.CostEstimate(flops=2 * terms * cols * depth**2, bytes_accessed=2 * terms * depth**2, transcendentals=0),
    )(place, facts, count, right, *pieces)


def whole_kernel(place_ref, facts, count_ref, *rest):
    rights_in, lefts_in, pieces = rest[0], rest[1], rest[2:20]
    out_ref, panels, rights, lefts, panel_sems, sems = rest[20:]
    share, _, rows, _ = panels.shape
    place = place_ref[0]
    copies = []
    for j in range(NZ):
        home = lax.rem(place + j, NZ)
        copies.append(pltpu.make_async_copy(rights_in.at[j], rights.at[:, pl.ds(j * rows, rows), :], sems.at[0, j]))
        copies.append(pltpu.make_async_copy(lefts_in.at[home], lefts.at[:, :, pl.ds(j * rows, rows)], sems.at[1, j]))
    for copy in copies:
        copy.start()
    for t in range(share):
        fetch(place * share + t, t, facts, pieces, panels, panel_sems)
    for copy in copies:
        copy.wait()
    for t in range(share):
        fetched(t, pieces, panels, panel_sems)
        image = product(panels[t], rights[t], place * share + t < count_ref[0])
        value = jnp.dot(lefts[t], image, preferred_element_type=F32)
        if t == 0:
            out_ref[...] = value
        else:
            out_ref[...] += value


def whole_terms(place, facts, count, rights, lefts, pieces):
    _, share, rows, depth = rights.shape
    return pl.pallas_call(
        whole_kernel,
        out_shape=jax.ShapeDtypeStruct((depth, depth), F32),
        in_specs=[SMEM] * 3 + [ANY] * 20,
        out_specs=VMEM,
        scratch_shapes=[
            pltpu.VMEM((share, NZ, rows, depth), BF16),
            pltpu.VMEM((share, depth, depth), BF16),
            pltpu.VMEM((share, depth, depth), BF16),
            pltpu.SemaphoreType.DMA((share, 2)),
            pltpu.SemaphoreType.DMA((2, NZ)),
        ],
        compiler_params=PARAMS,
        cost_estimate=pl.CostEstimate(flops=4 * share * depth**3, bytes_accessed=6 * share * depth**2, transcendentals=0),
    )(place, facts, count, rights, lefts, *pieces)


def gather_kernel(first, left_ref, sum_ref, images, out_ref, lefts, moved, sems):
    _, terms, rows, cols = images.shape
    copies = [
        pltpu.make_async_copy(left_ref.at[first + t], lefts.at[:, pl.ds(t * rows, rows)], sems.at[t]) for t in range(terms)
    ]
    for copy in copies:
        copy.start()
    for j in range(NZ):
        moved[:, j * cols : (j + 1) * cols] = images[j].reshape(terms * rows, cols)
    for copy in copies:
        copy.wait()
    for e in range(NZ):
        span = slice(e * rows, (e + 1) * rows)
        value = sum_ref[span, :] + jnp.dot(lefts[span, :], moved[...], preferred_element_type=F32)
        out_ref[e] = value.astype(out_ref.dtype)


def gather_terms(first, left, total, images):
    _, terms, rows, cols = images.shape
    width = total.shape[1]
    return pl.pallas_call(
        functools.partial(gather_kernel, first),
        out_shape=jax.ShapeDtypeStruct((NZ, rows, width), WIRE),
        in_specs=[ANY, VMEM, VMEM],
        out_specs=VMEM,
        scratch_shapes=[
            pltpu.VMEM((total.shape[0], terms * rows), BF16),
            pltpu.VMEM((terms * rows, width), BF16),
            pltpu.SemaphoreType.DMA((terms,)),
        ],
        compiler_params=PARAMS,
        cost_estimate=pl.CostEstimate(flops=2 * terms * rows * width**2, bytes_accessed=4 * width**2, transcendentals=0),
    )(left, total, images)


def final_kernel(place_ref, limit_ref, parts, out_ref):
    shape = out_ref.shape
    value = parts[0].astype(F32)
    for source in range(1, NZ):
        value = value + parts[source].astype(F32)
    row_ids = place_ref[0] * shape[0] + lax.broadcasted_iota(jnp.int32, shape, 0)
    col_ids = lax.broadcasted_iota(jnp.int32, shape, 1)
    inside = (row_ids < limit_ref[0]) & (col_ids < limit_ref[1])
    out_ref[...] = jnp.where(inside, value, jnp.zeros_like(value)).astype(BF16)


def body(psi, left_ops, right_ops, sources, counts, dims_left, dims_right):
    rows, width = psi.shape[1:]
    right, left = right_ops[:, 0], left_ops[:, 0]
    x, l, y, c, place = (lax.axis_index(name) for name in ("x", "l", "y", "c", "z"))
    row_ids = place * rows + lax.broadcasted_iota(jnp.int32, (rows, width), 0)
    col_ids = lax.broadcasted_iota(jnp.int32, (rows, width), 1)
    inside = (row_ids < dims_left[0]) & (col_ids < dims_right[0])
    panel = jnp.where(inside, psi[0], jnp.zeros_like(psi[0]))[None]
    place_in = place.astype(jnp.int32)[None]

    pair = jnp.concatenate([panel, swap(panel, "l")], axis=0)
    others = [from_op(pair, j) for j in range(1, NZ)]
    own = jnp.concatenate([pair] + [along(pair, 0, step) for step in (1, 2, 3)], axis=0)
    own_up, own_down = along(own, 1, 1), along(own, 1, 3)
    half = own.shape[0] // 2
    own_across = [along(own_up[:half], 1, 1), along(own_down[half:], 1, 3)]
    own = jnp.concatenate([own, own_up, own_down] + own_across, axis=0)
    own_there = swap(own, "c")
    stack = jnp.stack(others, axis=1).reshape(NL * (NZ - 1), rows, width)
    near = [stack] + [along(stack, 0, step) for step in (1, 2, 3)]
    low = jnp.concatenate(near[:2], axis=0)
    high = after(jnp.concatenate(near[2:], axis=0), *own_across)
    up_low, down_high = along(low, 1, 1), along(high, 1, 3)

    first = SHARE * NZ
    right_late = after(right[:first], *others)
    rights = lax.all_to_all(right_late.reshape(NZ, SHARE, rows, width), "z", 0, 0, tiled=True)
    left_late = after(left[:first], rights)
    lefts = lax.all_to_all(left_late.reshape(NZ, SHARE, width, rows), "z", 0, 0, tiled=True)

    up_high, down_low = along(high, 1, 1), along(low, 1, 3)
    a, b, *_ = lax.optimization_barrier((up_low, down_high, rights, own_there))
    across_low, across_high = along(a, 1, 1), along(b, 1, 3)
    early = [swap(piece, "c") for piece in (low, high, up_low, up_high, down_low, down_high)]
    c_low, c_high, *_ = lax.optimization_barrier((across_low, across_high, lefts, *early))
    others_here = [low, high, up_low, up_high, across_low, across_high, down_low, down_high]
    others_there = early[:4] + [swap(c_low, "c"), swap(c_high, "c")] + early[4:]
    pieces = [own, own_there] + others_here + others_there

    s = sources[0]
    sx, sl, sy, sc = s // (NL * NY * NC), s // (NY * NC) % NL, s // NC % NY, s % NC
    dx, dl, dy, dc = (sx - x) % NX, (sl - l) % NL, (sy - y) % NY, (sc - c) % NC
    near, far = jnp.where(sc == 0, dy, dx), jnp.where(sc == 0, dx, dy)
    own_slot = (jnp.where(far == 2, 3, jnp.where(far == 3, 2, far)) * 4 + near) * NL + dl
    piece = far * 2 + near // 2 + 8 * dc
    slot = (near % 2 * NL + dl) * (NZ - 1)
    facts = jnp.stack([dc, own_slot, piece, slot]).astype(jnp.int32)

    images = moving_products(first, place_in, facts, counts, right, pieces)
    total = whole_terms(place_in, after(facts, images), counts, rights, lefts, pieces)
    images = lax.all_to_all(images, "z", 0, 0, tiled=True)
    parts = lax.all_to_all(gather_terms(first, left, total, images), "z", 0, 0, tiled=True)
    limits = jnp.concatenate([dims_left, dims_right])
    return pl.pallas_call(
        final_kernel,
        out_shape=jax.ShapeDtypeStruct((rows, width), BF16),
        in_specs=[SMEM] * 2 + [VMEM],
        out_specs=VMEM,
    )(place_in, limits, parts)[None]


def solution(mesh):
    parts = Mesh(mesh.devices.reshape(NX, NL, NY, NC, NZ), SEC + ("z",))
    return jax.shard_map(
        body,
        mesh=parts,
        in_specs=(
            P(SEC, "z", None),
            P(None, SEC, None, "z"),
            P(None, SEC, "z", None),
            P(SEC, None),
            P(SEC),
            P(SEC),
            P(SEC),
        ),
        out_specs=P(SEC, "z", None),
        check_vma=False,
    )
```

time: 406 us -> 234 us (0.58)
  waiting for transfers between devices: 369 us -> 132 us
  starting transfers between devices: 0.08 us -> 60.4 us
  Pallas kernels: 0 us -> 15.5 us
  between operations: 15.4 us -> 2.47 us
  local copies, waits for them, and re-layouts: 8.46 us -> 20.2 us
  matrix products: 11.7 us -> 0 us
    all_gather x2 -> x0, waiting for transfers between devices: 337 us -> none  [the longest x1 220 us: body(): lax.all_gather(right_ops, 'op', axis=2, tiled=True)[:, 0]]
    ppermute x0 -> x29, waiting for transfers between devices: none -> 68.8 us  [the longest x16 46.1 us: along(): return lax.ppermute(value, ('x', 'y', 'c'), perm)]
    all_to_all x0 -> x4, waiting for transfers between devices: none -> 63 us  [the longest x1 28.4 us: body(): lax.all_to_all(left_late.reshape(NZ, SHARE, width, rows), 'z', 0, 0, tile...]
    ppermute x0 -> x29, starting transfers between devices: none -> 42.6 us  [the longest x16 23.6 us: along(): return lax.ppermute(value, ('x', 'y', 'c'), perm)]
    reduce_scatter x1 -> x0, waiting for transfers between devices: 31.7 us -> none  [body(): lax.psum_scatter(partial_sum[None], 'op', scatter_dimension=1, tiled=True)]
    all_to_all x0 -> x4, starting transfers between devices: none -> 17.9 us  [the longest x1 5.4 us: body(): lax.all_to_all(right_late.reshape(NZ, SHARE, rows, width), 'z', 0, 0, til...]
    pallas_call x0 -> x4, Pallas kernels: none -> 15.5 us  [the longest x1 5.94 us: whole_terms(): pl.pallas_call(whole_kernel, out_shape=jax.ShapeDtypeStruct((depth, depth...]
    unnamed x5 -> x31, local copies, waits for them, and re-layouts: 1.03 us -> 13.8 us
  transfers between devices with their start and end apart: 3 -> 33, of which waited for: 3 -> 19; matrix products, arithmetic and copies ran while one was open for 1% -> 6% of each run, Pallas kernels for 0% -> 3%
where the time goes in v1:
time: 234 us
  waiting for transfers between devices  132 us (56%)
  starting transfers between devices  60.4 us (26%)
  local copies, waits for them, and re-layouts  20.2 us (9%)
  Pallas kernels  15.5 us (7%)
  other arithmetic  3.25 us (1%)
  between operations  2.47 us (1%)
    ppermute x16, waiting for transfers between devices, along(): return lax.ppermute(value, ('x', 'y', 'c'), perm)  46.1 us
    all_to_all x1, waiting for transfers between devices, body(): lax.all_to_all(left_late.reshape(NZ, SHARE, width, rows), 'z', 0, 0, tile...  28.4 us
    ppermute x16, starting transfers between devices, along(): return lax.ppermute(value, ('x', 'y', 'c'), perm)  23.6 us
    all_to_all x1, waiting for transfers between devices, body(): images = lax.all_to_all(images, 'z', 0, 0, tiled=True)  19.7 us
    unnamed x31, local copies, waits for them, and re-layouts  13.8 us
    all_to_all x1, waiting for transfers between devices, body(): lax.all_to_all(gather_terms(first, left, total, images), 'z', 0, 0, tiled...  12.7 us
    ppermute x3, waiting for transfers between devices, from_op(): return lax.ppermute(value, 'z', [((z + step) % NZ, z) for z in range(NZ)])  11.8 us
    ppermute x10, waiting for transfers between devices, swap(): return lax.ppermute(value, axis, [(0, 1), (1, 0)])  11 us
  transfers between devices with their start and end apart: 33, of which 19 were waited for; matrix products, arithmetic and copies ran while one was open for 6% of the time, Pallas kernels for 3%

profile of v1, /device:TPU:1, one launch (start us, length us, event | category | flops | bytes accessed | tf_op | source)
XLA Modules:
  0.0 233.7 jit_solution(16936916410644698071)
XLA Ops:
  2.7 2.6 %collective-permute-start = (bf16[1,128,512]{2,1,0:T(8,128)(2,1)S(1)}, bf16[1,128,512]{2,1,0:T(8,128)(2,1)S(1)}, u32[]{:S(2)}, u32[]{:S(2)}) collective-permute-start(bf16[1,128,512]{2,1,0:T(8,128)(2,1)S(1)} %get-tuple-element.22), channel_id=1, source_target_pairs={{0,32},{32,0},{1,33},{33,1},{2,34},{34,2},{3,35},{35,3},{4,36},{36... | collective-permute-start | bytes 393224 | tf_op jit(solution)/shard_map/ppermute | solution.py:35
  5.2 2.4 %collective-permute-done = bf16[1,128,512]{2,1,0:T(8,128)(2,1)S(1)} collective-permute-done((bf16[1,128,512]{2,1,0:T(8,128)(2,1)S(1)}, bf16[1,128,512]{2,1,0:T(8,128)(2,1)S(1)}, u32[]{:S(2)}, u32[]{:S(2)}) %collective-permute-start) | collective-permute-done | bytes 131104 | tf_op jit(solution)/shard_map/ppermute | solution.py:35
  7.6 3.3 %collective-permute-start.1 = (bf16[2,128,512]{2,1,0:T(8,128)(2,1)S(1)}, bf16[2,128,512]{2,1,0:T(8,128)(2,1)S(1)}, u32[]{:S(2)}, u32[]{:S(2)}) collective-permute-start(bf16[2,128,512]{2,1,0:T(8,128)(2,1)S(1)} %pad_maximum_fusion.3), channel_id=1, source_target_pairs={{8,0},{68,4},{16,8},{76,12},{24,16},{84,20},{0,24},{92,28},{72,64}... | collective-permute-start | bytes 786440 | tf_op jit(solution)/shard_map/ppermute | solution.py:31
  13.4 3.7 %collective-permute-done.1 = bf16[2,128,512]{2,1,0:T(8,128)(2,1)S(1)} collective-permute-done((bf16[2,128,512]{2,1,0:T(8,128)(2,1)S(1)}, bf16[2,128,512]{2,1,0:T(8,128)(2,1)S(1)}, u32[]{:S(2)}, u32[]{:S(2)}) %collective-permute-start.1) | collective-permute-done | bytes 262176 | tf_op jit(solution)/shard_map/ppermute | solution.py:31
  21.5 2.4 %collective-permute-start.4 = (bf16[8,128,512]{2,1,0:T(8,128)(2,1)S(1)}, bf16[8,128,512]{2,1,0:T(8,128)(2,1)S(1)}, u32[]{:S(2)}, u32[]{:S(2)}) collective-permute-start(bf16[8,128,512]{2,1,0:T(8,128)(2,1)S(1)} %get-tuple-element.30), channel_id=1, source_target_pairs={{64,0},{12,4},{72,8},{20,12},{80,16},{28,20},{88,24},{4,28},{128,6... | collective-permute-start | bytes 3145736 | tf_op jit(solution)/shard_map/ppermute | solution.py:31
  23.9 3.0 %collective-permute-start.11 = (bf16[2,128,512]{2,1,0:T(8,128)(2,1)S(1)}, bf16[2,128,512]{2,1,0:T(8,128)(2,1)S(1)}, u32[]{:S(2)}, u32[]{:S(2)}) collective-permute-start(bf16[2,128,512]{2,1,0:T(8,128)(2,1)S(1)} %pad_maximum_fusion.3), channel_id=1, source_target_pairs={{3,0},{0,1},{1,2},{2,3},{7,4},{4,5},{5,6},{6,7},{11,8},{8,9},{9,10... | collective-permute-start | bytes 786440 | tf_op jit(solution)/shard_map/ppermute | solution.py:39
  26.9 4.7 %collective-permute-start.10 = (bf16[2,128,512]{2,1,0:T(8,128)(2,1)S(1)}, bf16[2,128,512]{2,1,0:T(8,128)(2,1)S(1)}, u32[]{:S(2)}, u32[]{:S(2)}) collective-permute-start(bf16[2,128,512]{2,1,0:T(8,128)(2,1)S(1)} %pad_maximum_fusion.3), channel_id=1, source_target_pairs={{2,0},{3,1},{0,2},{1,3},{6,4},{7,5},{4,6},{5,7},{10,8},{11,9},{8,1... | collective-permute-start | bytes 786440 | tf_op jit(solution)/shard_map/ppermute | solution.py:39
  31.6 2.4 %collective-permute-start.9 = (bf16[2,128,512]{2,1,0:T(8,128)(2,1)S(1)}, bf16[2,128,512]{2,1,0:T(8,128)(2,1)S(1)}, u32[]{:S(2)}, u32[]{:S(2)}) collective-permute-start(bf16[2,128,512]{2,1,0:T(8,128)(2,1)S(1)} %pad_maximum_fusion.3), channel_id=1, source_target_pairs={{1,0},{2,1},{3,2},{0,3},{5,4},{6,5},{7,6},{4,7},{9,8},{10,9},{11,1... | collective-permute-start | bytes 786440 | tf_op jit(solution)/shard_map/ppermute | solution.py:39
  37.5 3.4 %collective-permute-start.6 = (bf16[4,128,512]{2,1,0:T(8,128)(2,1)}, bf16[4,128,512]{2,1,0:T(8,128)(2,1)}, u32[]{:S(2)}, u32[]{:S(2)}) collective-permute-start(bf16[4,128,512]{2,1,0:T(8,128)(2,1)} %slice.24), channel_id=1, source_target_pairs={{64,0},{12,4},{72,8},{20,12},{80,16},{28,20},{88,24},{4,28},{128,6... | collective-permute-start | bytes 1572872 | tf_op jit(solution)/shard_map/ppermute | solution.py:31
  43.4 3.4 %collective-permute-done.10 = bf16[2,128,512]{2,1,0:T(8,128)(2,1)S(1)} collective-permute-done((bf16[2,128,512]{2,1,0:T(8,128)(2,1)S(1)}, bf16[2,128,512]{2,1,0:T(8,128)(2,1)S(1)}, u32[]{:S(2)}, u32[]{:S(2)}) %collective-permute-start.10) | collective-permute-done | bytes 262176 | tf_op jit(solution)/shard_map/ppermute | solution.py:39
  46.7 8.4 %collective-permute-done.9 = bf16[2,128,512]{2,1,0:T(8,128)(2,1)S(1)} collective-permute-done((bf16[2,128,512]{2,1,0:T(8,128)(2,1)S(1)}, bf16[2,128,512]{2,1,0:T(8,128)(2,1)S(1)}, u32[]{:S(2)}, u32[]{:S(2)}) %collective-permute-start.9) | collective-permute-done | bytes 262176 | tf_op jit(solution)/shard_map/ppermute | solution.py:39
  56.9 5.4 %all-to-all-start = ((bf16[4,4,128,512]{3,2,1,0:T(8,128)(2,1)}), bf16[4,4,128,512]{3,2,1,0:T(8,128)(2,1)}, u32[]{:S(2)}, u32[]{:S(2)}) async-start(bf16[4,4,128,512]{3,2,1,0:T(8,128)(2,1)} %bitcast.10), calls=%async_computation | async-start | bytes 4194304 | tf_op jit(solution)/shard_map/all_to_all | solution.py:236
  67.2 2.9 %collective-permute-start.8 = (bf16[32,128,512]{2,1,0:T(8,128)(2,1)}, bf16[32,128,512]{2,1,0:T(8,128)(2,1)}, u32[]{:S(2)}, u32[]{:S(2)}) collective-permute-start(bf16[32,128,512]{2,1,0:T(8,128)(2,1)} %constant_dynamic-update-slice_fusion.5.rest_0_.rest_2_), channel_id=1, source_target_pairs={{0,4},{4,0},{1,5},{5,1},{2,6},{6,2},{3,7},{7,3},{8,12},{12,8},{9,1... | collective-permute-start | bytes 12582920 | tf_op jit(solution)/shard_map/ppermute | solution.py:35
  70.1 2.7 %collective-permute-start.13 = (bf16[6,128,512]{2,1,0:T(8,128)(2,1)S(1)}, bf16[6,128,512]{2,1,0:T(8,128)(2,1)S(1)}, u32[]{:S(2)}, u32[]{:S(2)}) collective-permute-start(bf16[6,128,512]{2,1,0:T(8,128)(2,1)S(1)} %bitcast.23), channel_id=1, source_target_pairs={{16,0},{132,4},{24,8},{140,12},{0,16},{148,20},{8,24},{156,28},{80... | collective-permute-start | bytes 2359304 | tf_op jit(solution)/shard_map/ppermute | solution.py:31
  74.3 2.7 %collective-permute-start.15 = (bf16[12,128,512]{2,1,0:T(8,128)(2,1)S(1)}, bf16[12,128,512]{2,1,0:T(8,128)(2,1)}, u32[]{:S(2)}, u32[]{:S(2)}) collective-permute-start(bf16[12,128,512]{2,1,0:T(8,128)(2,1)S(1)} %pad_maximum_fusion.rest_2_.rest_4_), channel_id=1, source_target_pairs={{64,0},{12,4},{72,8},{20,12},{80,16},{28,20},{88,24},{4,28},{128,6... | collective-permute-start | bytes 4718600 | tf_op jit(solution)/shard_map/ppermute | solution.py:31
  77.0 9.8 %collective-permute-done.14 = bf16[6,128,512]{2,1,0:T(8,128)(2,1)S(1)} collective-permute-done((bf16[6,128,512]{2,1,0:T(8,128)(2,1)S(1)}, bf16[6,128,512]{2,1,0:T(8,128)(2,1)S(1)}, u32[]{:S(2)}, u32[]{:S(2)}) %collective-permute-start.14) | collective-permute-done | bytes 786464 | tf_op jit(solution)/shard_map/ppermute | solution.py:31
  86.7 17.5 %collective-permute-done.13 = bf16[6,128,512]{2,1,0:T(8,128)(2,1)S(1)} collective-permute-done((bf16[6,128,512]{2,1,0:T(8,128)(2,1)S(1)}, bf16[6,128,512]{2,1,0:T(8,128)(2,1)S(1)}, u32[]{:S(2)}, u32[]{:S(2)}) %collective-permute-start.13) | collective-permute-done | bytes 786464 | tf_op jit(solution)/shard_map/ppermute | solution.py:31
  106.1 2.3 all-to-all-done.rest_0_
  108.8 2.9 %collective-permute-start.16 = (bf16[12,128,512]{2,1,0:T(8,128)(2,1)S(1)}, bf16[12,128,512]{2,1,0:T(8,128)(2,1)}, u32[]{:S(2)}, u32[]{:S(2)}) collective-permute-start(bf16[12,128,512]{2,1,0:T(8,128)(2,1)S(1)} %pad_maximum_fusion.1.rest_3_.rest_5_), channel_id=1, source_target_pairs={{64,0},{12,4},{72,8},{20,12},{80,16},{28,20},{88,24},{4,28},{128,6... | collective-permute-start | bytes 4718600 | tf_op jit(solution)/shard_map/ppermute | solution.py:31
  111.7 4.6 %all-to-all-start.1 = ((bf16[4,4,512,128]{3,2,1,0:T(8,128)(2,1)}), bf16[4,4,512,128]{3,2,1,0:T(8,128)(2,1)}, u32[]{:S(2)}, u32[]{:S(2)}) async-start(bf16[4,4,512,128]{3,2,1,0:T(8,128)(2,1)} %bitcast.20), calls=%async_computation.1 | async-start | bytes 4194304 | tf_op jit(solution)/shard_map/all_to_all | solution.py:238
  116.4 9.0 %collective-permute-done.17.rest_9_.rest_11_ = bf16[12,128,512]{2,1,0:T(8,128)(2,1)} collective-permute-done((bf16[12,128,512]{2,1,0:T(8,128)(2,1)S(1)}, bf16[12,128,512]{2,1,0:T(8,128)(2,1)}, u32[]{:S(2)}, u32[]{:S(2)}) %collective-permute-start.17) | collective-permute-done | bytes 1572896 | tf_op jit(solution)/shard_map/ppermute | solution.py:31
  126.8 2.3 collective-permute-done.16.rest_5_.rest_7_
  129.4 3.2 %collective-permute-start.18 = (bf16[12,128,512]{2,1,0:T(8,128)(2,1)}, bf16[12,128,512]{2,1,0:T(8,128)(2,1)}, u32[]{:S(2)}, u32[]{:S(2)}) collective-permute-start(bf16[12,128,512]{2,1,0:T(8,128)(2,1)} %collective-permute-done.15.rest_4_.rest_6_), channel_id=1, source_target_pairs={{64,0},{12,4},{72,8},{20,12},{80,16},{28,20},{88,24},{4,28},{128,6... | collective-permute-start | bytes 4718600 | tf_op jit(solution)/shard_map/ppermute | solution.py:31
  136.4 28.4 %all-to-all-done.1.rest_1_ = bf16[4,4,512,128]{3,2,1,0:T(8,128)(2,1)} async-done(((bf16[4,4,512,128]{3,2,1,0:T(8,128)(2,1)}), bf16[4,4,512,128]{3,2,1,0:T(8,128)(2,1)}, u32[]{:S(2)}, u32[]{:S(2)}) %all-to-all-start.1) | async-done | bytes 2097184 | tf_op jit(solution)/shard_map/all_to_all | solution.py:238
  166.6 2.5 %collective-permute-done.27.rest_14_.rest_16_ = bf16[12,128,512]{2,1,0:T(8,128)(2,1)} collective-permute-done((bf16[12,128,512]{2,1,0:T(8,128)(2,1)}, bf16[12,128,512]{2,1,0:T(8,128)(2,1)}, u32[]{:S(2)}, u32[]{:S(2)}) %collective-permute-start.27) | collective-permute-done | bytes 1572896 | tf_op jit(solution)/shard_map/ppermute | solution.py:35
  171.3 4.4 %shard_map.73 = bf16[4,8,128,128]{3,2,1,0:T(8,128)(2,1)S(1)} custom-call(s32[1]{0:T(128)} %bitcast.place_ref, s32[4,24]{1,0:T(4,128)S(1)} %pad_add_fusion.facts, s32[1]{0:T(128)S(6)} %copy.21.count_ref, bf16[24,128,512]{2,1,0:T(8,128)(2,1)} %bitcast.19, bf16[32,128,512]{2,1,0:T(8,128)(2,1)} %constant_dynamic-update-slice_fusion.5.rest_0_.rest_2_, ...), custom_call_target="tpu_custom_call" | custom-call | flops 536870912 | bytes 4194304 | tf_op jit(solution)/shard_map/pallas_call | solution.py:103
  176.8 4.3 %all-to-all-start.2 = ((bf16[4,8,128,128]{3,2,1,0:T(8,128)(2,1)}), bf16[4,8,128,128]{3,2,1,0:T(8,128)(2,1)}, u32[]{:S(2)}, u32[]{:S(2)}) async-start(bf16[4,8,128,128]{3,2,1,0:T(8,128)(2,1)} %copy-done.2), calls=%async_computation.2 | async-start | bytes 2097152 | tf_op jit(solution)/shard_map/all_to_all | solution.py:260
  181.1 5.9 %shard_map.74.sum_ref = f32[512,512]{1,0:T(8,128)S(1)} custom-call(s32[1]{0:T(128)} %bitcast.place_ref, s32[4,24]{1,0:T(4,128)S(1)} %pad_add_fusion.facts, s32[1]{0:T(128)S(6)} %copy.21.count_ref, bf16[4,4,128,512]{3,2,1,0:T(8,128)(2,1)} %all-to-all-done.rest_0_, bf16[4,4,512,128]{3,2,1,0:T(8,128)(2,1)} %all-to-all-done.1.rest_1_, ...), custom_call_target="tpu_custom_call" | custom-call | flops 2147483648 | bytes 6291456 | tf_op jit(solution)/shard_map/pallas_call | solution.py:147
  188.0 19.7 %all-to-all-done.2.images = bf16[4,8,128,128]{3,2,1,0:T(8,128)(2,1)} async-done(((bf16[4,8,128,128]{3,2,1,0:T(8,128)(2,1)}), bf16[4,8,128,128]{3,2,1,0:T(8,128)(2,1)}, u32[]{:S(2)}, u32[]{:S(2)}) %all-to-all-start.2) | async-done | bytes 1048608 | tf_op jit(solution)/shard_map/all_to_all | solution.py:260
  210.8 3.3 %shard_map.75 = bf16[4,128,512]{2,1,0:T(8,128)(2,1)} custom-call(bf16[24,512,128]{2,1,0:T(8,128)(2,1)S(1)} %bitcast.18, f32[512,512]{1,0:T(8,128)S(1)} %copy-done.4, bf16[4,8,128,128]{3,2,1,0:T(8,128)(2,1)} %all-to-all-done.2.images), custom_call_target="tpu_custom_call" | custom-call | flops 536870912 | bytes 1048576 | tf_op jit(solution)/shard_map/pallas_call | solution.py:184
  214.2 3.6 %all-to-all-start.3 = ((bf16[4,128,512]{2,1,0:T(8,128)(2,1)}), bf16[4,128,512]{2,1,0:T(8,128)(2,1)S(1)}, u32[]{:S(2)}, u32[]{:S(2)}) async-start(bf16[4,128,512]{2,1,0:T(8,128)(2,1)} %shard_map.75), calls=%async_computation.3 | async-start | bytes 1048576 | tf_op jit(solution)/shard_map/all_to_all | solution.py:261
  218.4 12.7 %all-to-all-done.3.parts = bf16[4,128,512]{2,1,0:T(8,128)(2,1)S(1)} async-done(((bf16[4,128,512]{2,1,0:T(8,128)(2,1)}), bf16[4,128,512]{2,1,0:T(8,128)(2,1)S(1)}, u32[]{:S(2)}, u32[]{:S(2)}) %all-to-all-start.3) | async-done | bytes 524320 | tf_op jit(solution)/shard_map/all_to_all | solution.py:261
  (87 shorter events, 41.6 us)
Async XLA Ops:
  2.7 4.9 %collective-permute-start = (bf16[1,128,512]{2,1,0:T(8,128)(2,1)S(1)}, bf16[1,128,512]{2,1,0:T(8,128)(2,1)S(1)}, u32[]{:S(2)}, u32[]{:S(2)}) collective-permute-start(bf16[1,128,512]{2,1,0:T(8,128)(2,1)S(1)} %get-tuple-element.22), channel_id=1, source_target_pairs={{0,32},{32,0},{1,33},{33,1},{2,34},{34,2},{3,35},{35,3},{4,36},{36... | collective-permute-start | bytes 393224 | tf_op jit(solution)/shard_map/ppermute | solution.py:35
  7.6 9.4 %collective-permute-start.1 = (bf16[2,128,512]{2,1,0:T(8,128)(2,1)S(1)}, bf16[2,128,512]{2,1,0:T(8,128)(2,1)S(1)}, u32[]{:S(2)}, u32[]{:S(2)}) collective-permute-start(bf16[2,128,512]{2,1,0:T(8,128)(2,1)S(1)} %pad_maximum_fusion.3), channel_id=1, source_target_pairs={{8,0},{68,4},{16,8},{76,12},{24,16},{84,20},{0,24},{92,28},{72,64}... | collective-permute-start | bytes 786440 | tf_op jit(solution)/shard_map/ppermute | solution.py:31
  10.9 7.1 %collective-permute-start.2 = (bf16[2,128,512]{2,1,0:T(8,128)(2,1)S(1)}, bf16[2,128,512]{2,1,0:T(8,128)(2,1)S(1)}, u32[]{:S(2)}, u32[]{:S(2)}) collective-permute-start(bf16[2,128,512]{2,1,0:T(8,128)(2,1)S(1)} %pad_maximum_fusion.3), channel_id=1, source_target_pairs={{16,0},{132,4},{24,8},{140,12},{0,16},{148,20},{8,24},{156,28},{80... | collective-permute-start | bytes 786440 | tf_op jit(solution)/shard_map/ppermute | solution.py:31
  12.1 8.6 %collective-permute-start.3 = (bf16[2,128,512]{2,1,0:T(8,128)(2,1)S(1)}, bf16[2,128,512]{2,1,0:T(8,128)(2,1)S(1)}, u32[]{:S(2)}, u32[]{:S(2)}) collective-permute-start(bf16[2,128,512]{2,1,0:T(8,128)(2,1)S(1)} %pad_maximum_fusion.3), channel_id=1, source_target_pairs={{24,0},{196,4},{0,8},{204,12},{8,16},{212,20},{16,24},{220,28},{88... | collective-permute-start | bytes 786440 | tf_op jit(solution)/shard_map/ppermute | solution.py:31
  21.5 14.2 %collective-permute-start.4 = (bf16[8,128,512]{2,1,0:T(8,128)(2,1)S(1)}, bf16[8,128,512]{2,1,0:T(8,128)(2,1)S(1)}, u32[]{:S(2)}, u32[]{:S(2)}) collective-permute-start(bf16[8,128,512]{2,1,0:T(8,128)(2,1)S(1)} %get-tuple-element.30), channel_id=1, source_target_pairs={{64,0},{12,4},{72,8},{20,12},{80,16},{28,20},{88,24},{4,28},{128,6... | collective-permute-start | bytes 3145736 | tf_op jit(solution)/shard_map/ppermute | solution.py:31
  23.9 18.6 %collective-permute-start.5 = (bf16[8,128,512]{2,1,0:T(8,128)(2,1)S(1)}, bf16[8,128,512]{2,1,0:T(8,128)(2,1)S(1)}, u32[]{:S(2)}, u32[]{:S(2)}) collective-permute-start(bf16[8,128,512]{2,1,0:T(8,128)(2,1)S(1)} %get-tuple-element.30), channel_id=1, source_target_pairs={{192,0},{28,4},{200,8},{4,12},{208,16},{12,20},{216,24},{20,28},{0... | collective-permute-start | bytes 3145736 | tf_op jit(solution)/shard_map/ppermute | solution.py:31
  23.9 19.5 %collective-permute-start.11 = (bf16[2,128,512]{2,1,0:T(8,128)(2,1)S(1)}, bf16[2,128,512]{2,1,0:T(8,128)(2,1)S(1)}, u32[]{:S(2)}, u32[]{:S(2)}) collective-permute-start(bf16[2,128,512]{2,1,0:T(8,128)(2,1)S(1)} %pad_maximum_fusion.3), channel_id=1, source_target_pairs={{3,0},{0,1},{1,2},{2,3},{7,4},{4,5},{5,6},{6,7},{11,8},{8,9},{9,10... | collective-permute-start | bytes 786440 | tf_op jit(solution)/shard_map/ppermute | solution.py:39
  26.9 19.8 %collective-permute-start.10 = (bf16[2,128,512]{2,1,0:T(8,128)(2,1)S(1)}, bf16[2,128,512]{2,1,0:T(8,128)(2,1)S(1)}, u32[]{:S(2)}, u32[]{:S(2)}) collective-permute-start(bf16[2,128,512]{2,1,0:T(8,128)(2,1)S(1)} %pad_maximum_fusion.3), channel_id=1, source_target_pairs={{2,0},{3,1},{0,2},{1,3},{6,4},{7,5},{4,6},{5,7},{10,8},{11,9},{8,1... | collective-permute-start | bytes 786440 | tf_op jit(solution)/shard_map/ppermute | solution.py:39
  31.6 23.5 %collective-permute-start.9 = (bf16[2,128,512]{2,1,0:T(8,128)(2,1)S(1)}, bf16[2,128,512]{2,1,0:T(8,128)(2,1)S(1)}, u32[]{:S(2)}, u32[]{:S(2)}) collective-permute-start(bf16[2,128,512]{2,1,0:T(8,128)(2,1)S(1)} %pad_maximum_fusion.3), channel_id=1, source_target_pairs={{1,0},{2,1},{3,2},{0,3},{5,4},{6,5},{7,6},{4,7},{9,8},{10,9},{11,1... | collective-permute-start | bytes 786440 | tf_op jit(solution)/shard_map/ppermute | solution.py:39
  37.5 27.0 %collective-permute-start.6 = (bf16[4,128,512]{2,1,0:T(8,128)(2,1)}, bf16[4,128,512]{2,1,0:T(8,128)(2,1)}, u32[]{:S(2)}, u32[]{:S(2)}) collective-permute-start(bf16[4,128,512]{2,1,0:T(8,128)(2,1)} %slice.24), channel_id=1, source_target_pairs={{64,0},{12,4},{72,8},{20,12},{80,16},{28,20},{88,24},{4,28},{128,6... | collective-permute-start | bytes 1572872 | tf_op jit(solution)/shard_map/ppermute | solution.py:31
  43.4 23.0 %collective-permute-start.7 = (bf16[4,128,512]{2,1,0:T(8,128)(2,1)}, bf16[4,128,512]{2,1,0:T(8,128)(2,1)S(1)}, u32[]{:S(2)}, u32[]{:S(2)}) collective-permute-start(bf16[4,128,512]{2,1,0:T(8,128)(2,1)} %slice.25), channel_id=1, source_target_pairs={{192,0},{28,4},{200,8},{4,12},{208,16},{12,20},{216,24},{20,28},{0... | collective-permute-start | bytes 1572872 | tf_op jit(solution)/shard_map/ppermute | solution.py:31
  55.3 17.5 %collective-permute-start.12 = (bf16[6,128,512]{2,1,0:T(8,128)(2,1)S(1)}, bf16[6,128,512]{2,1,0:T(8,128)(2,1)}, u32[]{:S(2)}, u32[]{:S(2)}) collective-permute-start(bf16[6,128,512]{2,1,0:T(8,128)(2,1)S(1)} %bitcast.21), channel_id=1, source_target_pairs={{8,0},{68,4},{16,8},{76,12},{24,16},{84,20},{0,24},{92,28},{72,64}... | collective-permute-start | bytes 2359304 | tf_op jit(solution)/shard_map/ppermute | solution.py:31
  56.9 51.5 %all-to-all-start = ((bf16[4,4,128,512]{3,2,1,0:T(8,128)(2,1)}), bf16[4,4,128,512]{3,2,1,0:T(8,128)(2,1)}, u32[]{:S(2)}, u32[]{:S(2)}) async-start(bf16[4,4,128,512]{3,2,1,0:T(8,128)(2,1)} %bitcast.10), calls=%async_computation | async-start | bytes 4194304 | tf_op jit(solution)/shard_map/all_to_all | solution.py:236
  67.2 59.1 %collective-permute-start.8 = (bf16[32,128,512]{2,1,0:T(8,128)(2,1)}, bf16[32,128,512]{2,1,0:T(8,128)(2,1)}, u32[]{:S(2)}, u32[]{:S(2)}) collective-permute-start(bf16[32,128,512]{2,1,0:T(8,128)(2,1)} %constant_dynamic-update-slice_fusion.5.rest_0_.rest_2_), channel_id=1, source_target_pairs={{0,4},{4,0},{1,5},{5,1},{2,6},{6,2},{3,7},{7,3},{8,12},{12,8},{9,1... | collective-permute-start | bytes 12582920 | tf_op jit(solution)/shard_map/ppermute | solution.py:35
  70.1 16.6 %collective-permute-start.14 = (bf16[6,128,512]{2,1,0:T(8,128)(2,1)S(1)}, bf16[6,128,512]{2,1,0:T(8,128)(2,1)S(1)}, u32[]{:S(2)}, u32[]{:S(2)}) collective-permute-start(bf16[6,128,512]{2,1,0:T(8,128)(2,1)S(1)} %bitcast.22), channel_id=1, source_target_pairs={{24,0},{196,4},{0,8},{204,12},{8,16},{212,20},{16,24},{220,28},{88... | collective-permute-start | bytes 2359304 | tf_op jit(solution)/shard_map/ppermute | solution.py:31
  70.1 34.2 %collective-permute-start.13 = (bf16[6,128,512]{2,1,0:T(8,128)(2,1)S(1)}, bf16[6,128,512]{2,1,0:T(8,128)(2,1)S(1)}, u32[]{:S(2)}, u32[]{:S(2)}) collective-permute-start(bf16[6,128,512]{2,1,0:T(8,128)(2,1)S(1)} %bitcast.23), channel_id=1, source_target_pairs={{16,0},{132,4},{24,8},{140,12},{0,16},{148,20},{8,24},{156,28},{80... | collective-permute-start | bytes 2359304 | tf_op jit(solution)/shard_map/ppermute | solution.py:31
  74.0 34.3 %collective-permute-start.20 = (bf16[12,128,512]{2,1,0:T(8,128)(2,1)S(1)}, bf16[12,128,512]{2,1,0:T(8,128)(2,1)}, u32[]{:S(2)}, u32[]{:S(2)}) collective-permute-start(bf16[12,128,512]{2,1,0:T(8,128)(2,1)S(1)} %pad_maximum_fusion.rest_2_.rest_4_), channel_id=1, source_target_pairs={{192,0},{28,4},{200,8},{4,12},{208,16},{12,20},{216,24},{20,28},{0... | collective-permute-start | bytes 4718600 | tf_op jit(solution)/shard_map/ppermute | solution.py:31
  74.3 34.5 %collective-permute-start.15 = (bf16[12,128,512]{2,1,0:T(8,128)(2,1)S(1)}, bf16[12,128,512]{2,1,0:T(8,128)(2,1)}, u32[]{:S(2)}, u32[]{:S(2)}) collective-permute-start(bf16[12,128,512]{2,1,0:T(8,128)(2,1)S(1)} %pad_maximum_fusion.rest_2_.rest_4_), channel_id=1, source_target_pairs={{64,0},{12,4},{72,8},{20,12},{80,16},{28,20},{88,24},{4,28},{128,6... | collective-permute-start | bytes 4718600 | tf_op jit(solution)/shard_map/ppermute | solution.py:31
  104.4 21.0 %collective-permute-start.17 = (bf16[12,128,512]{2,1,0:T(8,128)(2,1)S(1)}, bf16[12,128,512]{2,1,0:T(8,128)(2,1)}, u32[]{:S(2)}, u32[]{:S(2)}) collective-permute-start(bf16[12,128,512]{2,1,0:T(8,128)(2,1)S(1)} %pad_maximum_fusion.1.rest_3_.rest_5_), channel_id=1, source_target_pairs={{192,0},{28,4},{200,8},{4,12},{208,16},{12,20},{216,24},{20,28},{0... | collective-permute-start | bytes 4718600 | tf_op jit(solution)/shard_map/ppermute | solution.py:31
  106.0 20.4 %collective-permute-start.21 = (bf16[12,128,512]{2,1,0:T(8,128)(2,1)S(1)}, bf16[12,128,512]{2,1,0:T(8,128)(2,1)}, u32[]{:S(2)}, u32[]{:S(2)}) collective-permute-start(bf16[12,128,512]{2,1,0:T(8,128)(2,1)S(1)} %pad_maximum_fusion.rest_2_.rest_4_), channel_id=1, source_target_pairs={{0,4},{4,0},{1,5},{5,1},{2,6},{6,2},{3,7},{7,3},{8,12},{12,8},{9,1... | collective-permute-start | bytes 4718600 | tf_op jit(solution)/shard_map/ppermute | solution.py:35
  108.3 21.1 %collective-permute-start.22 = (bf16[12,128,512]{2,1,0:T(8,128)(2,1)S(1)}, bf16[12,128,512]{2,1,0:T(8,128)(2,1)}, u32[]{:S(2)}, u32[]{:S(2)}) collective-permute-start(bf16[12,128,512]{2,1,0:T(8,128)(2,1)S(1)} %pad_maximum_fusion.1.rest_3_.rest_5_), channel_id=1, source_target_pairs={{0,4},{4,0},{1,5},{5,1},{2,6},{6,2},{3,7},{7,3},{8,12},{12,8},{9,1... | collective-permute-start | bytes 4718600 | tf_op jit(solution)/shard_map/ppermute | solution.py:35
  108.8 20.2 %collective-permute-start.16 = (bf16[12,128,512]{2,1,0:T(8,128)(2,1)S(1)}, bf16[12,128,512]{2,1,0:T(8,128)(2,1)}, u32[]{:S(2)}, u32[]{:S(2)}) collective-permute-start(bf16[12,128,512]{2,1,0:T(8,128)(2,1)S(1)} %pad_maximum_fusion.1.rest_3_.rest_5_), channel_id=1, source_target_pairs={{64,0},{12,4},{72,8},{20,12},{80,16},{28,20},{88,24},{4,28},{128,6... | collective-permute-start | bytes 4718600 | tf_op jit(solution)/shard_map/ppermute | solution.py:31
  111.7 53.1 %all-to-all-start.1 = ((bf16[4,4,512,128]{3,2,1,0:T(8,128)(2,1)}), bf16[4,4,512,128]{3,2,1,0:T(8,128)(2,1)}, u32[]{:S(2)}, u32[]{:S(2)}) async-start(bf16[4,4,512,128]{3,2,1,0:T(8,128)(2,1)} %bitcast.20), calls=%async_computation.1 | async-start | bytes 4194304 | tf_op jit(solution)/shard_map/all_to_all | solution.py:238
  125.3 7.3 %collective-permute-start.25 = (bf16[12,128,512]{2,1,0:T(8,128)(2,1)}, bf16[12,128,512]{2,1,0:T(8,128)(2,1)}, u32[]{:S(2)}, u32[]{:S(2)}) collective-permute-start(bf16[12,128,512]{2,1,0:T(8,128)(2,1)} %collective-permute-done.20.rest_8_.rest_10_), channel_id=1, source_target_pairs={{0,4},{4,0},{1,5},{5,1},{2,6},{6,2},{3,7},{7,3},{8,12},{12,8},{9,1... | collective-permute-start | bytes 4718600 | tf_op jit(solution)/shard_map/ppermute | solution.py:35
  126.3 6.3 %collective-permute-start.23 = (bf16[12,128,512]{2,1,0:T(8,128)(2,1)}, bf16[12,128,512]{2,1,0:T(8,128)(2,1)}, u32[]{:S(2)}, u32[]{:S(2)}) collective-permute-start(bf16[12,128,512]{2,1,0:T(8,128)(2,1)} %collective-permute-done.15.rest_4_.rest_6_), channel_id=1, source_target_pairs={{0,4},{4,0},{1,5},{5,1},{2,6},{6,2},{3,7},{7,3},{8,12},{12,8},{9,1... | collective-permute-start | bytes 4718600 | tf_op jit(solution)/shard_map/ppermute | solution.py:35
  126.3 7.9 %collective-permute-start.26 = (bf16[12,128,512]{2,1,0:T(8,128)(2,1)}, bf16[12,128,512]{2,1,0:T(8,128)(2,1)}, u32[]{:S(2)}, u32[]{:S(2)}) collective-permute-start(bf16[12,128,512]{2,1,0:T(8,128)(2,1)} %collective-permute-done.17.rest_9_.rest_11_), channel_id=1, source_target_pairs={{0,4},{4,0},{1,5},{5,1},{2,6},{6,2},{3,7},{7,3},{8,12},{12,8},{9,1... | collective-permute-start | bytes 4718600 | tf_op jit(solution)/shard_map/ppermute | solution.py:35
  129.1 7.3 %collective-permute-start.24 = (bf16[12,128,512]{2,1,0:T(8,128)(2,1)}, bf16[12,128,512]{2,1,0:T(8,128)(2,1)}, u32[]{:S(2)}, u32[]{:S(2)}) collective-permute-start(bf16[12,128,512]{2,1,0:T(8,128)(2,1)} %collective-permute-done.16.rest_5_.rest_7_), channel_id=1, source_target_pairs={{0,4},{4,0},{1,5},{5,1},{2,6},{6,2},{3,7},{7,3},{8,12},{12,8},{9,1... | collective-permute-start | bytes 4718600 | tf_op jit(solution)/shard_map/ppermute | solution.py:35
  129.4 35.4 %collective-permute-start.18 = (bf16[12,128,512]{2,1,0:T(8,128)(2,1)}, bf16[12,128,512]{2,1,0:T(8,128)(2,1)}, u32[]{:S(2)}, u32[]{:S(2)}) collective-permute-start(bf16[12,128,512]{2,1,0:T(8,128)(2,1)} %collective-permute-done.15.rest_4_.rest_6_), channel_id=1, source_target_pairs={{64,0},{12,4},{72,8},{20,12},{80,16},{28,20},{88,24},{4,28},{128,6... | collective-permute-start | bytes 4718600 | tf_op jit(solution)/shard_map/ppermute | solution.py:31
  132.6 32.2 %collective-permute-start.19 = (bf16[12,128,512]{2,1,0:T(8,128)(2,1)}, bf16[12,128,512]{2,1,0:T(8,128)(2,1)}, u32[]{:S(2)}, u32[]{:S(2)}) collective-permute-start(bf16[12,128,512]{2,1,0:T(8,128)(2,1)} %collective-permute-done.17.rest_9_.rest_11_), channel_id=1, source_target_pairs={{192,0},{28,4},{200,8},{4,12},{208,16},{12,20},{216,24},{20,28},{0... | collective-permute-start | bytes 4718600 | tf_op jit(solution)/shard_map/ppermute | solution.py:31
  165.7 5.6 %collective-permute-start.28 = (bf16[12,128,512]{2,1,0:T(8,128)(2,1)}, bf16[12,128,512]{2,1,0:T(8,128)(2,1)}, u32[]{:S(2)}, u32[]{:S(2)}) collective-permute-start(bf16[12,128,512]{2,1,0:T(8,128)(2,1)} %collective-permute-done.19.rest_7_.rest_9_), channel_id=1, source_target_pairs={{0,4},{4,0},{1,5},{5,1},{2,6},{6,2},{3,7},{7,3},{8,12},{12,8},{9,1... | collective-permute-start | bytes 4718600 | tf_op jit(solution)/shard_map/ppermute | solution.py:35
  176.8 30.9 %all-to-all-start.2 = ((bf16[4,8,128,128]{3,2,1,0:T(8,128)(2,1)}), bf16[4,8,128,128]{3,2,1,0:T(8,128)(2,1)}, u32[]{:S(2)}, u32[]{:S(2)}) async-start(bf16[4,8,128,128]{3,2,1,0:T(8,128)(2,1)} %copy-done.2), calls=%async_computation.2 | async-start | bytes 2097152 | tf_op jit(solution)/shard_map/all_to_all | solution.py:260
  214.2 16.9 %all-to-all-start.3 = ((bf16[4,128,512]{2,1,0:T(8,128)(2,1)}), bf16[4,128,512]{2,1,0:T(8,128)(2,1)S(1)}, u32[]{:S(2)}, u32[]{:S(2)}) async-start(bf16[4,128,512]{2,1,0:T(8,128)(2,1)} %shard_map.75), calls=%async_computation.3 | async-start | bytes 1048576 | tf_op jit(solution)/shard_map/all_to_all | solution.py:261
  (13 other events, 176.3 us)

commit v2 on v1

--- a/solution.py
+++ b/solution.py
@@ -11,7 +11,7 @@
 NX, NL, NY, NC, NZ = 4, 2, 4, 2, 4
 F32, BF16 = jnp.float32, jnp.bfloat16
 SEC = ("x", "l", "y", "c")
-SHARE = 4
+SHARE = 5
 WIRE = BF16
 VMEM_LIMIT = 40 * 1024 * 1024
 ANY = pl.BlockSpec(memory_space=pl.ANY)
@@ -117,15 +117,19 @@
 
 
 def whole_kernel(place_ref, facts, count_ref, *rest):
-    rights_in, lefts_in, pieces = rest[0], rest[1], rest[2:20]
-    out_ref, panels, rights, lefts, panel_sems, sems = rest[20:]
+    operators, pieces = rest[0], rest[1:19]
+    out_ref, panels, rights, lefts, panel_sems, sems = rest[19:]
     share, _, rows, _ = panels.shape
     place = place_ref[0]
     copies = []
     for j in range(NZ):
         home = lax.rem(place + j, NZ)
-        copies.append(pltpu.make_async_copy(rights_in.at[j], rights.at[:, pl.ds(j * rows, rows), :], sems.at[0, j]))
-        copies.append(pltpu.make_async_copy(lefts_in.at[home], lefts.at[:, :, pl.ds(j * rows, rows)], sems.at[1, j]))
+        there = rights.at[:, pl.ds(j * rows, rows), :]
+        copies.append(pltpu.make_async_copy(operators.at[j, pl.ds(0, share)], there, sems.at[NZ, j]))
+        for m in range(NZ):
+            here = operators.at[home, pl.ds(share, share), :, pl.ds(m * rows, rows)]
+            there = lefts.at[:, pl.ds(m * rows, rows), pl.ds(j * rows, rows)]
+            copies.append(pltpu.make_async_copy(here, there, sems.at[m, j]))
     for copy in copies:
         copy.start()
     for t in range(share):
@@ -142,23 +146,24 @@
             out_ref[...] += value
 
 
-def whole_terms(place, facts, count, rights, lefts, pieces):
-    _, share, rows, depth = rights.shape
+def whole_terms(place, facts, count, operators, pieces):
+    _, share, rows, depth = operators.shape
+    share //= 2
     return pl.pallas_call(
         whole_kernel,
         out_shape=jax.ShapeDtypeStruct((depth, depth), F32),
-        in_specs=[SMEM] * 3 + [ANY] * 20,
+        in_specs=[SMEM] * 3 + [ANY] * 19,
         out_specs=VMEM,
         scratch_shapes=[
             pltpu.VMEM((share, NZ, rows, depth), BF16),
             pltpu.VMEM((share, depth, depth), BF16),
             pltpu.VMEM((share, depth, depth), BF16),
             pltpu.SemaphoreType.DMA((share, 2)),
-            pltpu.SemaphoreType.DMA((2, NZ)),
+            pltpu.SemaphoreType.DMA((NZ + 1, NZ)),
         ],
         compiler_params=PARAMS,
         cost_estimate=pl.CostEstimate(flops=4 * share * depth**3, bytes_accessed=6 * share * depth**2, transcendentals=0),
-    )(place, facts, count, rights, lefts, *pieces)
+    )(place, facts, count, operators, *pieces)
 
 
 def gather_kernel(first, left_ref, sum_ref, images, out_ref, lefts, moved, sems):
@@ -219,29 +224,27 @@
 
     pair = jnp.concatenate([panel, swap(panel, "l")], axis=0)
     others = [from_op(pair, j) for j in range(1, NZ)]
+    first = SHARE * NZ
+    wide = jnp.concatenate([left[:first, m * rows : (m + 1) * rows] for m in range(NZ)], axis=2)
+    both = jnp.concatenate([v.reshape(NZ, SHARE, rows, width) for v in (right[:first], wide)], axis=1)
+    whole = lax.all_to_all(after(both, *others), "z", 0, 0, tiled=True)
     own = jnp.concatenate([pair] + [along(pair, 0, step) for step in (1, 2, 3)], axis=0)
     own_up, own_down = along(own, 1, 1), along(own, 1, 3)
     half = own.shape[0] // 2
     own_across = [along(own_up[:half], 1, 1), along(own_down[half:], 1, 3)]
     own = jnp.concatenate([own, own_up, own_down] + own_across, axis=0)
-    own_there = swap(own, "c")
+    own_there = swap(after(own, whole), "c")
     stack = jnp.stack(others, axis=1).reshape(NL * (NZ - 1), rows, width)
     near = [stack] + [along(stack, 0, step) for step in (1, 2, 3)]
     low = jnp.concatenate(near[:2], axis=0)
-    high = after(jnp.concatenate(near[2:], axis=0), *own_across)
+    high = jnp.concatenate(near[2:], axis=0)
     up_low, down_high = along(low, 1, 1), along(high, 1, 3)
 
-    first = SHARE * NZ
-    right_late = after(right[:first], *others)
-    rights = lax.all_to_all(right_late.reshape(NZ, SHARE, rows, width), "z", 0, 0, tiled=True)
-    left_late = after(left[:first], rights)
-    lefts = lax.all_to_all(left_late.reshape(NZ, SHARE, width, rows), "z", 0, 0, tiled=True)
-
     up_high, down_low = along(high, 1, 1), along(low, 1, 3)
-    a, b, *_ = lax.optimization_barrier((up_low, down_high, rights, own_there))
+    a, b, *_ = (up_low, down_high, None)
     across_low, across_high = along(a, 1, 1), along(b, 1, 3)
     early = [swap(piece, "c") for piece in (low, high, up_low, up_high, down_low, down_high)]
-    c_low, c_high, *_ = lax.optimization_barrier((across_low, across_high, lefts, *early))
+    c_low, c_high, *_ = lax.optimization_barrier((across_low, across_high, *early))
     others_here = [low, high, up_low, up_high, across_low, across_high, down_low, down_high]
     others_there = early[:4] + [swap(c_low, "c"), swap(c_high, "c")] + early[4:]
     pieces = [own, own_there] + others_here + others_there
@@ -256,7 +259,7 @@
     facts = jnp.stack([dc, own_slot, piece, slot]).astype(jnp.int32)
 
     images = moving_products(first, place_in, facts, counts, right, pieces)
-    total = whole_terms(place_in, after(facts, images), counts, rights, lefts, pieces)
+    total = whole_terms(place_in, after(facts, images), counts, whole, pieces)
     images = lax.all_to_all(images, "z", 0, 0, tiled=True)
     parts = lax.all_to_all(gather_terms(first, left, total, images), "z", 0, 0, tiled=True)
     limits = jnp.concatenate([dims_left, dims_right])

time: 234 us -> 232 us (level)
  the two profiles are of different devices: /device:TPU:1 before, /device:TPU:36 now
where the time goes in v2:
time: 232 us; the launch traced here: 231 us
  waiting for transfers between devices  136 us (59%)
  starting transfers between devices  53 us (23%)
  local copies, waits for them, and re-layouts  20.6 us (9%)
  Pallas kernels  14.4 us (6%)
  other arithmetic  5.74 us (2%)
    ppermute x16, waiting for transfers between devices, along(): return lax.ppermute(value, ('x', 'y', 'c'), perm)  67.4 us
    ppermute x16, starting transfers between devices, along(): return lax.ppermute(value, ('x', 'y', 'c'), perm)  21.1 us
    ppermute x10, waiting for transfers between devices, swap(): return lax.ppermute(value, axis, [(0, 1), (1, 0)])  20.6 us
    ppermute x3, waiting for transfers between devices, from_op(): return lax.ppermute(value, 'z', [((z + step) % NZ, z) for z in range(NZ)])  15.5 us
    unnamed x26, local copies, waits for them, and re-layouts  15.3 us
    all_to_all x1, waiting for transfers between devices, body(): lax.all_to_all(gather_terms(first, left, total, images), 'z', 0, 0, tiled...  14.8 us
    all_to_all x1, waiting for transfers between devices, body(): whole = lax.all_to_all(after(both, *others), 'z', 0, 0, tiled=True)  11.3 us
    all_to_all x1, starting transfers between devices, body(): images = lax.all_to_all(images, 'z', 0, 0, tiled=True)  9.81 us
  transfers between devices with their start and end apart: 32, of which 20 were waited for; matrix products, arithmetic and copies ran while one was open for 6% of the time, Pallas kernels for 3%

profile of v2, /device:TPU:36, one launch (start us, length us, event | category | flops | bytes accessed | tf_op | source)
XLA Modules:
  0.0 231.5 jit_solution(10935966542278741264)
XLA Ops:
  3.1 2.0 fusion.13
  5.1 3.1 %collective-permute-done = bf16[1,128,512]{2,1,0:T(8,128)(2,1)S(1)} collective-permute-done((bf16[1,128,512]{2,1,0:T(8,128)(2,1)S(1)}, bf16[1,128,512]{2,1,0:T(8,128)(2,1)S(1)}, u32[]{:S(2)}, u32[]{:S(2)}) %collective-permute-start) | collective-permute-done | bytes 131104 | tf_op jit(solution)/shard_map/ppermute | solution.py:35
  8.3 5.5 %collective-permute-start.8 = (bf16[2,128,512]{2,1,0:T(8,128)(2,1)S(1)}, bf16[2,128,512]{2,1,0:T(8,128)(2,1)S(1)}, u32[]{:S(2)}, u32[]{:S(2)}) collective-permute-start(bf16[2,128,512]{2,1,0:T(8,128)(2,1)S(1)} %pad_maximum_fusion.4), channel_id=1, source_target_pairs={{1,0},{2,1},{3,2},{0,3},{5,4},{6,5},{7,6},{4,7},{9,8},{10,9},{11,1... | collective-permute-start | bytes 786440 | tf_op jit(solution)/shard_map/ppermute | solution.py:39
  15.2 2.4 %collective-permute-start.10 = (bf16[2,128,512]{2,1,0:T(8,128)(2,1)S(1)}, bf16[2,128,512]{2,1,0:T(8,128)(2,1)S(1)}, u32[]{:S(2)}, u32[]{:S(2)}) collective-permute-start(bf16[2,128,512]{2,1,0:T(8,128)(2,1)S(1)} %pad_maximum_fusion.4), channel_id=1, source_target_pairs={{3,0},{0,1},{1,2},{2,3},{7,4},{4,5},{5,6},{6,7},{11,8},{8,9},{9,10... | collective-permute-start | bytes 786440 | tf_op jit(solution)/shard_map/ppermute | solution.py:39
  19.3 2.8 %pad_maximum_fusion = bf16[4,10,128,512]{3,2,1,0:T(8,128)(2,1)} fusion(bf16[4,5,128,512]{3,2,1,0:T(8,128)(2,1)S(1)} %bitcast.18, bf16[4,5,128,512]{3,2,1,0:T(8,128)(2,1)S(1)} %bitcast.17), kind=kLoop, calls=%fused_computation | loop fusion | flops 2621440 | bytes 10485760 | tf_op jit(solution)/shard_map/concatenate | solution.py:229
  22.1 7.6 %collective-permute-done.8 = bf16[2,128,512]{2,1,0:T(8,128)(2,1)S(1)} collective-permute-done((bf16[2,128,512]{2,1,0:T(8,128)(2,1)S(1)}, bf16[2,128,512]{2,1,0:T(8,128)(2,1)S(1)}, u32[]{:S(2)}, u32[]{:S(2)}) %collective-permute-start.8) | collective-permute-done | bytes 262176 | tf_op jit(solution)/shard_map/ppermute | solution.py:39
  29.8 7.4 %collective-permute-done.9 = bf16[2,128,512]{2,1,0:T(8,128)(2,1)S(1)} collective-permute-done((bf16[2,128,512]{2,1,0:T(8,128)(2,1)S(1)}, bf16[2,128,512]{2,1,0:T(8,128)(2,1)S(1)}, u32[]{:S(2)}, u32[]{:S(2)}) %collective-permute-start.9) | collective-permute-done | bytes 262176 | tf_op jit(solution)/shard_map/ppermute | solution.py:39
  37.7 6.8 %all-to-all-start = ((bf16[4,10,128,512]{3,2,1,0:T(8,128)(2,1)}), bf16[4,10,128,512]{3,2,1,0:T(8,128)(2,1)}, u32[]{:S(2)}, u32[]{:S(2)}) async-start(bf16[4,10,128,512]{3,2,1,0:T(8,128)(2,1)} %pad_maximum_fusion), calls=%async_computation | async-start | bytes 10485760 | tf_op jit(solution)/shard_map/all_to_all | solution.py:230
  44.5 3.0 %collective-permute-start.1 = (bf16[2,128,512]{2,1,0:T(8,128)(2,1)S(1)}, bf16[2,128,512]{2,1,0:T(8,128)(2,1)S(1)}, u32[]{:S(2)}, u32[]{:S(2)}) collective-permute-start(bf16[2,128,512]{2,1,0:T(8,128)(2,1)S(1)} %pad_maximum_fusion.4), channel_id=1, source_target_pairs={{8,0},{68,4},{16,8},{76,12},{24,16},{84,20},{0,24},{92,28},{72,64}... | collective-permute-start | bytes 786440 | tf_op jit(solution)/shard_map/ppermute | solution.py:31
  48.8 3.2 %collective-permute-start.13 = (bf16[6,128,512]{2,1,0:T(8,128)(2,1)S(1)}, bf16[6,128,512]{2,1,0:T(8,128)(2,1)S(1)}, u32[]{:S(2)}, u32[]{:S(2)}) collective-permute-start(bf16[6,128,512]{2,1,0:T(8,128)(2,1)S(1)} %bitcast.20), channel_id=1, source_target_pairs={{16,0},{132,4},{24,8},{140,12},{0,16},{148,20},{8,24},{156,28},{80... | collective-permute-start | bytes 2359304 | tf_op jit(solution)/shard_map/ppermute | solution.py:31
  57.2 10.4 %collective-permute-done.3 = bf16[2,128,512]{2,1,0:T(8,128)(2,1)S(1)} collective-permute-done((bf16[2,128,512]{2,1,0:T(8,128)(2,1)S(1)}, bf16[2,128,512]{2,1,0:T(8,128)(2,1)S(1)}, u32[]{:S(2)}, u32[]{:S(2)}) %collective-permute-start.3) | collective-permute-done | bytes 262176 | tf_op jit(solution)/shard_map/ppermute | solution.py:31
  71.3 10.2 %collective-permute-done.14 = bf16[6,128,512]{2,1,0:T(8,128)(2,1)S(1)} collective-permute-done((bf16[6,128,512]{2,1,0:T(8,128)(2,1)S(1)}, bf16[6,128,512]{2,1,0:T(8,128)(2,1)S(1)}, u32[]{:S(2)}, u32[]{:S(2)}) %collective-permute-start.14) | collective-permute-done | bytes 786464 | tf_op jit(solution)/shard_map/ppermute | solution.py:31
  84.3 1.8 collective-permute-start.20
  86.1 36.7 %collective-permute-done.6 = bf16[4,128,512]{2,1,0:T(8,128)(2,1)S(1)} collective-permute-done((bf16[4,128,512]{2,1,0:T(8,128)(2,1)S(1)}, bf16[4,128,512]{2,1,0:T(8,128)(2,1)S(1)}, u32[]{:S(2)}, u32[]{:S(2)}) %collective-permute-start.6) | collective-permute-done | bytes 524320 | tf_op jit(solution)/shard_map/ppermute | solution.py:31
  122.8 2.4 %collective-permute-start.7 = (bf16[4,128,512]{2,1,0:T(8,128)(2,1)S(1)}, bf16[4,128,512]{2,1,0:T(8,128)(2,1)S(1)}, u32[]{:S(2)}, u32[]{:S(2)}) collective-permute-start(bf16[4,128,512]{2,1,0:T(8,128)(2,1)S(1)} %slice.30), channel_id=1, source_target_pairs={{192,0},{28,4},{200,8},{4,12},{208,16},{12,20},{216,24},{20,28},{0... | collective-permute-start | bytes 1572872 | tf_op jit(solution)/shard_map/ppermute | solution.py:31
  125.2 6.8 %collective-permute-done.7 = bf16[4,128,512]{2,1,0:T(8,128)(2,1)S(1)} collective-permute-done((bf16[4,128,512]{2,1,0:T(8,128)(2,1)S(1)}, bf16[4,128,512]{2,1,0:T(8,128)(2,1)S(1)}, u32[]{:S(2)}, u32[]{:S(2)}) %collective-permute-start.7) | collective-permute-done | bytes 524320 | tf_op jit(solution)/shard_map/ppermute | solution.py:31
  133.6 2.4 %collective-permute-start.19 = (bf16[12,128,512]{2,1,0:T(8,128)(2,1)}, bf16[12,128,512]{2,1,0:T(8,128)(2,1)}, u32[]{:S(2)}, u32[]{:S(2)}) collective-permute-start(bf16[12,128,512]{2,1,0:T(8,128)(2,1)} %collective-permute-done.18.rest_9_.rest_10_), channel_id=1, source_target_pairs={{192,0},{28,4},{200,8},{4,12},{208,16},{12,20},{216,24},{20,28},{0... | collective-permute-start | bytes 4718600 | tf_op jit(solution)/shard_map/ppermute | solution.py:31
  139.9 11.3 %all-to-all-done.rest_0_ = bf16[4,10,128,512]{3,2,1,0:T(8,128)(2,1)} async-done(((bf16[4,10,128,512]{3,2,1,0:T(8,128)(2,1)}), bf16[4,10,128,512]{3,2,1,0:T(8,128)(2,1)}, u32[]{:S(2)}, u32[]{:S(2)}) %all-to-all-start) | async-done | bytes 5242912 | tf_op jit(solution)/shard_map/all_to_all | solution.py:230
  155.0 6.0 %collective-permute-done.23.rest_12_.rest_13_ = bf16[12,128,512]{2,1,0:T(8,128)(2,1)} collective-permute-done((bf16[12,128,512]{2,1,0:T(8,128)(2,1)}, bf16[12,128,512]{2,1,0:T(8,128)(2,1)}, u32[]{:S(2)}, u32[]{:S(2)}) %collective-permute-start.23) | collective-permute-done | bytes 1572896 | tf_op jit(solution)/shard_map/ppermute | solution.py:35
  161.0 2.2 collective-permute-done.24.rest_13_.rest_14_
  163.2 2.2 collective-permute-done.25.rest_16_.rest_17_
  165.5 2.2 collective-permute-done.26.rest_17_.rest_18_
  169.0 2.5 %collective-permute-done.27.rest_14_.rest_15_ = bf16[12,128,512]{2,1,0:T(8,128)(2,1)} collective-permute-done((bf16[12,128,512]{2,1,0:T(8,128)(2,1)}, bf16[12,128,512]{2,1,0:T(8,128)(2,1)}, u32[]{:S(2)}, u32[]{:S(2)}) %collective-permute-start.27) | collective-permute-done | bytes 1572896 | tf_op jit(solution)/shard_map/ppermute | solution.py:35
  171.5 2.2 collective-permute-done.28.rest_15_.rest_16_
  175.2 2.9 %shard_map.73 = bf16[4,4,128,128]{3,2,1,0:T(8,128)(2,1)S(1)} custom-call(s32[1]{0:T(128)} %bitcast.place_ref, s32[4,24]{1,0:T(4,128)S(1)} %pad_add_fusion.facts, s32[1]{0:T(128)S(6)} %copy.22.count_ref, bf16[24,128,512]{2,1,0:T(8,128)(2,1)} %bitcast.16, bf16[32,128,512]{2,1,0:T(8,128)(2,1)} %constant_dynamic-update-slice_fusion.5.rest_0_.rest_1_, ...), custom_call_target="tpu_custom_call" | custom-call | flops 268435456 | bytes 2097152 | tf_op jit(solution)/shard_map/pallas_call | solution.py:103
  178.9 9.8 %all-to-all-start.1 = ((bf16[4,4,128,128]{3,2,1,0:T(8,128)(2,1)}), bf16[4,4,128,128]{3,2,1,0:T(8,128)(2,1)}, u32[]{:S(2)}, u32[]{:S(2)}) async-start(bf16[4,4,128,128]{3,2,1,0:T(8,128)(2,1)} %copy-done.6), calls=%async_computation.1 | async-start | bytes 1048576 | tf_op jit(solution)/shard_map/all_to_all | solution.py:263
  190.1 7.2 %shard_map.74.sum_ref = f32[512,512]{1,0:T(8,128)S(1)} custom-call(s32[1]{0:T(128)} %bitcast.place_ref, s32[4,24]{1,0:T(4,128)S(1)} %pad_add_fusion.facts, s32[1]{0:T(128)S(6)} %copy.22.count_ref, bf16[4,10,128,512]{3,2,1,0:T(8,128)(2,1)} %all-to-all-done.rest_0_, bf16[32,128,512]{2,1,0:T(8,128)(2,1)} %constant_dynamic-update-slice_fusion.5.rest_0_.rest_1_, ...), custom_call_target="tpu_custom_call" | custom-call | flops 2684354560 | bytes 7864320 | tf_op jit(solution)/shard_map/pallas_call | solution.py:152
  198.3 6.0 %all-to-all-done.1.images = bf16[4,4,128,128]{3,2,1,0:T(8,128)(2,1)} async-done(((bf16[4,4,128,128]{3,2,1,0:T(8,128)(2,1)}), bf16[4,4,128,128]{3,2,1,0:T(8,128)(2,1)}, u32[]{:S(2)}, u32[]{:S(2)}) %all-to-all-start.1) | async-done | bytes 524320 | tf_op jit(solution)/shard_map/all_to_all | solution.py:263
  204.3 1.9 copy-done
  207.4 2.5 %shard_map.75 = bf16[4,128,512]{2,1,0:T(8,128)(2,1)} custom-call(bf16[24,512,128]{2,1,0:T(8,128)(2,1)S(1)} %bitcast.15, f32[512,512]{1,0:T(8,128)S(1)} %copy-done.5, bf16[4,4,128,128]{3,2,1,0:T(8,128)(2,1)} %all-to-all-done.1.images), custom_call_target="tpu_custom_call" | custom-call | flops 268435456 | bytes 1048576 | tf_op jit(solution)/shard_map/pallas_call | solution.py:189
  209.9 3.6 %all-to-all-start.2 = ((bf16[4,128,512]{2,1,0:T(8,128)(2,1)}), bf16[4,128,512]{2,1,0:T(8,128)(2,1)S(1)}, u32[]{:S(2)}, u32[]{:S(2)}) async-start(bf16[4,128,512]{2,1,0:T(8,128)(2,1)} %shard_map.75), calls=%async_computation.2 | async-start | bytes 1048576 | tf_op jit(solution)/shard_map/all_to_all | solution.py:264
  214.1 14.8 %all-to-all-done.2.parts = bf16[4,128,512]{2,1,0:T(8,128)(2,1)S(1)} async-done(((bf16[4,128,512]{2,1,0:T(8,128)(2,1)}), bf16[4,128,512]{2,1,0:T(8,128)(2,1)S(1)}, u32[]{:S(2)}, u32[]{:S(2)}) %all-to-all-start.2) | async-done | bytes 524320 | tf_op jit(solution)/shard_map/all_to_all | solution.py:264
  (83 shorter events, 37.3 us)
Async XLA Ops:
  3.0 5.2 %collective-permute-start = (bf16[1,128,512]{2,1,0:T(8,128)(2,1)S(1)}, bf16[1,128,512]{2,1,0:T(8,128)(2,1)S(1)}, u32[]{:S(2)}, u32[]{:S(2)}) collective-permute-start(bf16[1,128,512]{2,1,0:T(8,128)(2,1)S(1)} %get-tuple-element.16), channel_id=1, source_target_pairs={{0,32},{32,0},{1,33},{33,1},{2,34},{34,2},{3,35},{35,3},{4,36},{36... | collective-permute-start | bytes 393224 | tf_op jit(solution)/shard_map/ppermute | solution.py:35
  8.3 21.5 %collective-permute-start.8 = (bf16[2,128,512]{2,1,0:T(8,128)(2,1)S(1)}, bf16[2,128,512]{2,1,0:T(8,128)(2,1)S(1)}, u32[]{:S(2)}, u32[]{:S(2)}) collective-permute-start(bf16[2,128,512]{2,1,0:T(8,128)(2,1)S(1)} %pad_maximum_fusion.4), channel_id=1, source_target_pairs={{1,0},{2,1},{3,2},{0,3},{5,4},{6,5},{7,6},{4,7},{9,8},{10,9},{11,1... | collective-permute-start | bytes 786440 | tf_op jit(solution)/shard_map/ppermute | solution.py:39
  13.7 23.5 %collective-permute-start.9 = (bf16[2,128,512]{2,1,0:T(8,128)(2,1)S(1)}, bf16[2,128,512]{2,1,0:T(8,128)(2,1)S(1)}, u32[]{:S(2)}, u32[]{:S(2)}) collective-permute-start(bf16[2,128,512]{2,1,0:T(8,128)(2,1)S(1)} %pad_maximum_fusion.4), channel_id=1, source_target_pairs={{2,0},{3,1},{0,2},{1,3},{6,4},{7,5},{4,6},{5,7},{10,8},{11,9},{8,1... | collective-permute-start | bytes 786440 | tf_op jit(solution)/shard_map/ppermute | solution.py:39
  15.2 22.5 %collective-permute-start.10 = (bf16[2,128,512]{2,1,0:T(8,128)(2,1)S(1)}, bf16[2,128,512]{2,1,0:T(8,128)(2,1)S(1)}, u32[]{:S(2)}, u32[]{:S(2)}) collective-permute-start(bf16[2,128,512]{2,1,0:T(8,128)(2,1)S(1)} %pad_maximum_fusion.4), channel_id=1, source_target_pairs={{3,0},{0,1},{1,2},{2,3},{7,4},{4,5},{5,6},{6,7},{11,8},{8,9},{9,10... | collective-permute-start | bytes 786440 | tf_op jit(solution)/shard_map/ppermute | solution.py:39
  37.7 113.5 %all-to-all-start = ((bf16[4,10,128,512]{3,2,1,0:T(8,128)(2,1)}), bf16[4,10,128,512]{3,2,1,0:T(8,128)(2,1)}, u32[]{:S(2)}, u32[]{:S(2)}) async-start(bf16[4,10,128,512]{3,2,1,0:T(8,128)(2,1)} %pad_maximum_fusion), calls=%async_computation | async-start | bytes 10485760 | tf_op jit(solution)/shard_map/all_to_all | solution.py:230
  44.5 9.5 %collective-permute-start.1 = (bf16[2,128,512]{2,1,0:T(8,128)(2,1)S(1)}, bf16[2,128,512]{2,1,0:T(8,128)(2,1)S(1)}, u32[]{:S(2)}, u32[]{:S(2)}) collective-permute-start(bf16[2,128,512]{2,1,0:T(8,128)(2,1)S(1)} %pad_maximum_fusion.4), channel_id=1, source_target_pairs={{8,0},{68,4},{16,8},{76,12},{24,16},{84,20},{0,24},{92,28},{72,64}... | collective-permute-start | bytes 786440 | tf_op jit(solution)/shard_map/ppermute | solution.py:31
  47.7 22.8 %collective-permute-start.12 = (bf16[6,128,512]{2,1,0:T(8,128)(2,1)S(1)}, bf16[6,128,512]{2,1,0:T(8,128)(2,1)S(1)}, u32[]{:S(2)}, u32[]{:S(2)}) collective-permute-start(bf16[6,128,512]{2,1,0:T(8,128)(2,1)S(1)} %bitcast.19), channel_id=1, source_target_pairs={{8,0},{68,4},{16,8},{76,12},{24,16},{84,20},{0,24},{92,28},{72,64}... | collective-permute-start | bytes 2359304 | tf_op jit(solution)/shard_map/ppermute | solution.py:31
  48.5 7.9 %collective-permute-start.2 = (bf16[2,128,512]{2,1,0:T(8,128)(2,1)S(1)}, bf16[2,128,512]{2,1,0:T(8,128)(2,1)S(1)}, u32[]{:S(2)}, u32[]{:S(2)}) collective-permute-start(bf16[2,128,512]{2,1,0:T(8,128)(2,1)S(1)} %pad_maximum_fusion.4), channel_id=1, source_target_pairs={{16,0},{132,4},{24,8},{140,12},{0,16},{148,20},{8,24},{156,28},{80... | collective-permute-start | bytes 786440 | tf_op jit(solution)/shard_map/ppermute | solution.py:31
  48.8 22.4 %collective-permute-start.13 = (bf16[6,128,512]{2,1,0:T(8,128)(2,1)S(1)}, bf16[6,128,512]{2,1,0:T(8,128)(2,1)S(1)}, u32[]{:S(2)}, u32[]{:S(2)}) collective-permute-start(bf16[6,128,512]{2,1,0:T(8,128)(2,1)S(1)} %bitcast.20), channel_id=1, source_target_pairs={{16,0},{132,4},{24,8},{140,12},{0,16},{148,20},{8,24},{156,28},{80... | collective-permute-start | bytes 2359304 | tf_op jit(solution)/shard_map/ppermute | solution.py:31
  52.7 14.9 %collective-permute-start.3 = (bf16[2,128,512]{2,1,0:T(8,128)(2,1)S(1)}, bf16[2,128,512]{2,1,0:T(8,128)(2,1)S(1)}, u32[]{:S(2)}, u32[]{:S(2)}) collective-permute-start(bf16[2,128,512]{2,1,0:T(8,128)(2,1)S(1)} %pad_maximum_fusion.4), channel_id=1, source_target_pairs={{24,0},{196,4},{0,8},{204,12},{8,16},{212,20},{16,24},{220,28},{88... | collective-permute-start | bytes 786440 | tf_op jit(solution)/shard_map/ppermute | solution.py:31
  54.0 27.5 %collective-permute-start.14 = (bf16[6,128,512]{2,1,0:T(8,128)(2,1)S(1)}, bf16[6,128,512]{2,1,0:T(8,128)(2,1)S(1)}, u32[]{:S(2)}, u32[]{:S(2)}) collective-permute-start(bf16[6,128,512]{2,1,0:T(8,128)(2,1)S(1)} %bitcast.21), channel_id=1, source_target_pairs={{24,0},{196,4},{0,8},{204,12},{8,16},{212,20},{16,24},{220,28},{88... | collective-permute-start | bytes 2359304 | tf_op jit(solution)/shard_map/ppermute | solution.py:31
  68.4 15.3 %collective-permute-start.4 = (bf16[8,128,512]{2,1,0:T(8,128)(2,1)}, bf16[8,128,512]{2,1,0:T(8,128)(2,1)S(1)}, u32[]{:S(2)}, u32[]{:S(2)}) collective-permute-start(bf16[8,128,512]{2,1,0:T(8,128)(2,1)} %get-tuple-element.28), channel_id=1, source_target_pairs={{64,0},{12,4},{72,8},{20,12},{80,16},{28,20},{88,24},{4,28},{128,6... | collective-permute-start | bytes 3145736 | tf_op jit(solution)/shard_map/ppermute | solution.py:31
  69.0 15.3 %collective-permute-start.5 = (bf16[8,128,512]{2,1,0:T(8,128)(2,1)}, bf16[8,128,512]{2,1,0:T(8,128)(2,1)S(1)}, u32[]{:S(2)}, u32[]{:S(2)}) collective-permute-start(bf16[8,128,512]{2,1,0:T(8,128)(2,1)} %get-tuple-element.28), channel_id=1, source_target_pairs={{192,0},{28,4},{200,8},{4,12},{208,16},{12,20},{216,24},{20,28},{0... | collective-permute-start | bytes 3145736 | tf_op jit(solution)/shard_map/ppermute | solution.py:31
  70.6 61.6 %collective-permute-start.15 = (bf16[12,128,512]{2,1,0:T(8,128)(2,1)S(1)}, bf16[12,128,512]{2,1,0:T(8,128)(2,1)}, u32[]{:S(2)}, u32[]{:S(2)}) collective-permute-start(bf16[12,128,512]{2,1,0:T(8,128)(2,1)S(1)} %pad_maximum_fusion.2.rest_2_.rest_3_), channel_id=1, source_target_pairs={{64,0},{12,4},{72,8},{20,12},{80,16},{28,20},{88,24},{4,28},{128,6... | collective-permute-start | bytes 4718600 | tf_op jit(solution)/shard_map/ppermute | solution.py:31
  81.6 50.9 %collective-permute-start.16 = (bf16[12,128,512]{2,1,0:T(8,128)(2,1)S(1)}, bf16[12,128,512]{2,1,0:T(8,128)(2,1)S(1)}, u32[]{:S(2)}, u32[]{:S(2)}) collective-permute-start(bf16[12,128,512]{2,1,0:T(8,128)(2,1)S(1)} %constant_dynamic-update-slice_fusion.14.rest_3_.rest_4_), channel_id=1, source_target_pairs={{64,0},{12,4},{72,8},{20,12},{80,16},{28,20},{88,24},{4,28},{128,6... | collective-permute-start | bytes 4718600 | tf_op jit(solution)/shard_map/ppermute | solution.py:31
  82.1 50.9 %collective-permute-start.18 = (bf16[12,128,512]{2,1,0:T(8,128)(2,1)S(1)}, bf16[12,128,512]{2,1,0:T(8,128)(2,1)}, u32[]{:S(2)}, u32[]{:S(2)}) collective-permute-start(bf16[12,128,512]{2,1,0:T(8,128)(2,1)S(1)} %constant_dynamic-update-slice_fusion.14.rest_3_.rest_4_), channel_id=1, source_target_pairs={{192,0},{28,4},{200,8},{4,12},{208,16},{12,20},{216,24},{20,28},{0... | collective-permute-start | bytes 4718600 | tf_op jit(solution)/shard_map/ppermute | solution.py:31
  83.7 39.0 %collective-permute-start.6 = (bf16[4,128,512]{2,1,0:T(8,128)(2,1)S(1)}, bf16[4,128,512]{2,1,0:T(8,128)(2,1)S(1)}, u32[]{:S(2)}, u32[]{:S(2)}) collective-permute-start(bf16[4,128,512]{2,1,0:T(8,128)(2,1)S(1)} %slice.29), channel_id=1, source_target_pairs={{64,0},{12,4},{72,8},{20,12},{80,16},{28,20},{88,24},{4,28},{128,6... | collective-permute-start | bytes 1572872 | tf_op jit(solution)/shard_map/ppermute | solution.py:31
  84.3 67.0 %collective-permute-start.20 = (bf16[12,128,512]{2,1,0:T(8,128)(2,1)S(1)}, bf16[12,128,512]{2,1,0:T(8,128)(2,1)}, u32[]{:S(2)}, u32[]{:S(2)}) collective-permute-start(bf16[12,128,512]{2,1,0:T(8,128)(2,1)S(1)} %pad_maximum_fusion.2.rest_2_.rest_3_), channel_id=1, source_target_pairs={{192,0},{28,4},{200,8},{4,12},{208,16},{12,20},{216,24},{20,28},{0... | collective-permute-start | bytes 4718600 | tf_op jit(solution)/shard_map/ppermute | solution.py:31
  122.8 9.2 %collective-permute-start.7 = (bf16[4,128,512]{2,1,0:T(8,128)(2,1)S(1)}, bf16[4,128,512]{2,1,0:T(8,128)(2,1)S(1)}, u32[]{:S(2)}, u32[]{:S(2)}) collective-permute-start(bf16[4,128,512]{2,1,0:T(8,128)(2,1)S(1)} %slice.30), channel_id=1, source_target_pairs={{192,0},{28,4},{200,8},{4,12},{208,16},{12,20},{216,24},{20,28},{0... | collective-permute-start | bytes 1572872 | tf_op jit(solution)/shard_map/ppermute | solution.py:31
  132.0 19.3 %collective-permute-start.21 = (bf16[12,128,512]{2,1,0:T(8,128)(2,1)S(1)}, bf16[12,128,512]{2,1,0:T(8,128)(2,1)}, u32[]{:S(2)}, u32[]{:S(2)}) collective-permute-start(bf16[12,128,512]{2,1,0:T(8,128)(2,1)S(1)} %pad_maximum_fusion.2.rest_2_.rest_3_), channel_id=1, source_target_pairs={{0,4},{4,0},{1,5},{5,1},{2,6},{6,2},{3,7},{7,3},{8,12},{12,8},{9,1... | collective-permute-start | bytes 4718600 | tf_op jit(solution)/shard_map/ppermute | solution.py:35
  132.2 19.6 %collective-permute-start.22 = (bf16[12,128,512]{2,1,0:T(8,128)(2,1)S(1)}, bf16[12,128,512]{2,1,0:T(8,128)(2,1)}, u32[]{:S(2)}, u32[]{:S(2)}) collective-permute-start(bf16[12,128,512]{2,1,0:T(8,128)(2,1)S(1)} %constant_dynamic-update-slice_fusion.14.rest_3_.rest_4_), channel_id=1, source_target_pairs={{0,4},{4,0},{1,5},{5,1},{2,6},{6,2},{3,7},{7,3},{8,12},{12,8},{9,1... | collective-permute-start | bytes 4718600 | tf_op jit(solution)/shard_map/ppermute | solution.py:35
  132.5 21.1 %collective-permute-start.17 = (bf16[12,128,512]{2,1,0:T(8,128)(2,1)}, bf16[12,128,512]{2,1,0:T(8,128)(2,1)}, u32[]{:S(2)}, u32[]{:S(2)}) collective-permute-start(bf16[12,128,512]{2,1,0:T(8,128)(2,1)} %collective-permute-done.15.rest_4_.rest_5_), channel_id=1, source_target_pairs={{64,0},{12,4},{72,8},{20,12},{80,16},{28,20},{88,24},{4,28},{128,6... | collective-permute-start | bytes 4718600 | tf_op jit(solution)/shard_map/ppermute | solution.py:31
  133.6 20.7 %collective-permute-start.19 = (bf16[12,128,512]{2,1,0:T(8,128)(2,1)}, bf16[12,128,512]{2,1,0:T(8,128)(2,1)}, u32[]{:S(2)}, u32[]{:S(2)}) collective-permute-start(bf16[12,128,512]{2,1,0:T(8,128)(2,1)} %collective-permute-done.18.rest_9_.rest_10_), channel_id=1, source_target_pairs={{192,0},{28,4},{200,8},{4,12},{208,16},{12,20},{216,24},{20,28},{0... | collective-permute-start | bytes 4718600 | tf_op jit(solution)/shard_map/ppermute | solution.py:31
  151.2 22.5 %collective-permute-start.11 = (bf16[32,128,512]{2,1,0:T(8,128)(2,1)}, bf16[32,128,512]{2,1,0:T(8,128)(2,1)}, u32[]{:S(2)}, u32[]{:S(2)}) collective-permute-start(bf16[32,128,512]{2,1,0:T(8,128)(2,1)} %constant_dynamic-update-slice_fusion.5.rest_0_.rest_1_), channel_id=1, source_target_pairs={{0,4},{4,0},{1,5},{5,1},{2,6},{6,2},{3,7},{7,3},{8,12},{12,8},{9,1... | collective-permute-start | bytes 12582920 | tf_op jit(solution)/shard_map/ppermute | solution.py:35
  151.2 9.7 %collective-permute-start.23 = (bf16[12,128,512]{2,1,0:T(8,128)(2,1)}, bf16[12,128,512]{2,1,0:T(8,128)(2,1)}, u32[]{:S(2)}, u32[]{:S(2)}) collective-permute-start(bf16[12,128,512]{2,1,0:T(8,128)(2,1)} %collective-permute-done.15.rest_4_.rest_5_), channel_id=1, source_target_pairs={{0,4},{4,0},{1,5},{5,1},{2,6},{6,2},{3,7},{7,3},{8,12},{12,8},{9,1... | collective-permute-start | bytes 4718600 | tf_op jit(solution)/shard_map/ppermute | solution.py:35
  151.8 11.5 %collective-permute-start.24 = (bf16[12,128,512]{2,1,0:T(8,128)(2,1)}, bf16[12,128,512]{2,1,0:T(8,128)(2,1)}, u32[]{:S(2)}, u32[]{:S(2)}) collective-permute-start(bf16[12,128,512]{2,1,0:T(8,128)(2,1)} %copy-done.1), channel_id=1, source_target_pairs={{0,4},{4,0},{1,5},{5,1},{2,6},{6,2},{3,7},{7,3},{8,12},{12,8},{9,1... | collective-permute-start | bytes 4718600 | tf_op jit(solution)/shard_map/ppermute | solution.py:35
  153.6 11.9 %collective-permute-start.25 = (bf16[12,128,512]{2,1,0:T(8,128)(2,1)}, bf16[12,128,512]{2,1,0:T(8,128)(2,1)}, u32[]{:S(2)}, u32[]{:S(2)}) collective-permute-start(bf16[12,128,512]{2,1,0:T(8,128)(2,1)} %collective-permute-done.20.rest_8_.rest_9_), channel_id=1, source_target_pairs={{0,4},{4,0},{1,5},{5,1},{2,6},{6,2},{3,7},{7,3},{8,12},{12,8},{9,1... | collective-permute-start | bytes 4718600 | tf_op jit(solution)/shard_map/ppermute | solution.py:35
  154.4 13.4 %collective-permute-start.26 = (bf16[12,128,512]{2,1,0:T(8,128)(2,1)}, bf16[12,128,512]{2,1,0:T(8,128)(2,1)}, u32[]{:S(2)}, u32[]{:S(2)}) collective-permute-start(bf16[12,128,512]{2,1,0:T(8,128)(2,1)} %collective-permute-done.18.rest_9_.rest_10_), channel_id=1, source_target_pairs={{0,4},{4,0},{1,5},{5,1},{2,6},{6,2},{3,7},{7,3},{8,12},{12,8},{9,1... | collective-permute-start | bytes 4718600 | tf_op jit(solution)/shard_map/ppermute | solution.py:35
  167.7 3.8 %collective-permute-start.27 = (bf16[12,128,512]{2,1,0:T(8,128)(2,1)}, bf16[12,128,512]{2,1,0:T(8,128)(2,1)}, u32[]{:S(2)}, u32[]{:S(2)}) collective-permute-start(bf16[12,128,512]{2,1,0:T(8,128)(2,1)} %collective-permute-done.17.rest_6_.rest_7_), channel_id=1, source_target_pairs={{0,4},{4,0},{1,5},{5,1},{2,6},{6,2},{3,7},{7,3},{8,12},{12,8},{9,1... | collective-permute-start | bytes 4718600 | tf_op jit(solution)/shard_map/ppermute | solution.py:35
  167.9 5.9 %collective-permute-start.28 = (bf16[12,128,512]{2,1,0:T(8,128)(2,1)}, bf16[12,128,512]{2,1,0:T(8,128)(2,1)}, u32[]{:S(2)}, u32[]{:S(2)}) collective-permute-start(bf16[12,128,512]{2,1,0:T(8,128)(2,1)} %collective-permute-done.19.rest_7_.rest_8_), channel_id=1, source_target_pairs={{0,4},{4,0},{1,5},{5,1},{2,6},{6,2},{3,7},{7,3},{8,12},{12,8},{9,1... | collective-permute-start | bytes 4718600 | tf_op jit(solution)/shard_map/ppermute | solution.py:35
  178.9 25.4 %all-to-all-start.1 = ((bf16[4,4,128,128]{3,2,1,0:T(8,128)(2,1)}), bf16[4,4,128,128]{3,2,1,0:T(8,128)(2,1)}, u32[]{:S(2)}, u32[]{:S(2)}) async-start(bf16[4,4,128,128]{3,2,1,0:T(8,128)(2,1)} %copy-done.6), calls=%async_computation.1 | async-start | bytes 1048576 | tf_op jit(solution)/shard_map/all_to_all | solution.py:263
  209.9 19.0 %all-to-all-start.2 = ((bf16[4,128,512]{2,1,0:T(8,128)(2,1)}), bf16[4,128,512]{2,1,0:T(8,128)(2,1)S(1)}, u32[]{:S(2)}, u32[]{:S(2)}) async-start(bf16[4,128,512]{2,1,0:T(8,128)(2,1)} %shard_map.75), calls=%async_computation.2 | async-start | bytes 1048576 | tf_op jit(solution)/shard_map/all_to_all | solution.py:264
  (10 other events, 98.7 us)
